TPU v7x, 512 devices: a whole 4x4x16 slice. The times are simulated.
512 devices in a mesh: band: 16 (over z), space: 32 (over y, x, core).
Axes of the slice: x: 4, y: 4, z: 16, core: 2. Of those that a mesh axis runs over, the one named last changes fastest.
Arguments:
- orbitals: float32 [2, 64, 96, 9216], P(None, 'band', 'space'), may hold values from -6 to 6
- potential: float32 [96, 9216], P('space'), may hold values from -2 to 4
- occupations: float32 [64], P('band'), may hold values from 0.5 to 2
Outputs:
- propagated: float32 [2, 64, 96, 9216], P(None, 'band', 'space')
- density: float32 [96, 9216], P('space')
- hartree: float32 [96, 9216], P('space')
All inputs are finite; a program needn't handle non-finite values.
Results may differ from a plain program's by a relative error of at most 0.0029.
Values may be sent and summed in bfloat16 or wider, within the bound.
A program may use at most 64 MiB of HBM per device.

v0:
```python
import math

import jax
import jax.numpy as jnp
from jax import lax
from jax.sharding import PartitionSpec as P

NX = 96
NY = 96
NZ = 96


stencil_coeffs = (-205.0 / 72.0, 8.0 / 5.0, -1.0 / 5.0, 8.0 / 315.0, -1.0 / 560.0)
energy_shift = 6.0
energy_scale = 8.0
bessel_terms = (0.7651976865579666, 0.44005058574493355, 0.11490348493190049)


def from_behind(x, axis, by):
    count = lax.axis_size(axis)
    pairs = [(i, i + by) for i in range(count) if 0 <= i + by < count]
    return lax.ppermute(x, axis, pairs)


def over_pieces(x, axis):
    return lax.all_gather(x, axis).sum(0)


def plane_laplace(center, wider):
    reach_cells = len(stencil_coeffs) - 1
    planes = center.shape[-2]
    cells = center.shape[-1]
    spread = wider.astype(jnp.float32)
    middle = spread[..., reach_cells : reach_cells + planes, :]
    summed = 3.0 * stencil_coeffs[0] * center
    for offset in range(1, reach_cells + 1):
        after = spread[..., reach_cells + offset : reach_cells + offset + planes, :]
        before = spread[..., reach_cells - offset : reach_cells - offset + planes, :]
        summed = summed + stencil_coeffs[offset] * (after + before)
    margin = reach_cells * NZ
    padded = jnp.pad(middle, [(0, 0)] * (middle.ndim - 1) + [(margin, margin)])
    z_index = lax.iota(jnp.int32, cells) % NZ
    for offset in range(1, reach_cells + 1):
        stride = offset * NZ
        beyond = padded[..., margin + stride : margin + stride + cells]
        behind = padded[..., margin - stride : margin - stride + cells]
        summed = summed + stencil_coeffs[offset] * (beyond + behind)
        beyond = jnp.where(
            z_index + offset < NZ, padded[..., margin + offset : margin + offset + cells], 0.0
        )
        behind = jnp.where(
            z_index - offset >= 0, padded[..., margin - offset : margin - offset + cells], 0.0
        )
        summed = summed + stencil_coeffs[offset] * (beyond + behind)
    return summed


def scaled_hamiltonian(center, wider, field_values):
    energy = -0.5 * plane_laplace(center, wider) + field_values * center
    return (energy - energy_shift * center) / energy_scale


def slab_rims(source, extent):
    planes = source.shape[-2]
    lower_parts = []
    upper_parts = []
    for distance in range(1, -(-extent // planes) + 1):
        needed = min(planes, extent - (distance - 1) * planes)
        for heading in (1, -1):
            if heading == 1:
                outgoing = source[..., planes - needed :, :]
            else:
                outgoing = source[..., :needed, :]
            arrived = from_behind(outgoing, "space", heading * distance)
            if heading == 1:
                lower_parts.append(arrived)
            else:
                upper_parts.append(arrived)
    return jnp.concatenate(lower_parts[::-1] + [source] + upper_parts, axis=-2)


def dft_tables(length):
    indices = lax.iota(jnp.int32, length)
    product = indices[:, None] * indices[None, :] % length
    phases = 2.0 * math.pi / length * product.astype(jnp.float32)
    return (jnp.cos(phases), jnp.sin(phases))


def turn_axis(cosine, sines, values, pattern):
    direct = jnp.einsum(pattern, cosine, values, precision=lax.Precision.HIGHEST)
    crossed = jnp.einsum(pattern, sines, values, precision=lax.Precision.HIGHEST)
    real_part = direct[..., :NZ] - crossed[..., NZ:]
    imag_part = direct[..., NZ:] + crossed[..., :NZ]
    return jnp.concatenate([real_part, imag_part], axis=-1)


def squared_waves(length, anchor, extent):
    indices = anchor + lax.iota(jnp.int32, extent)
    signed = jnp.where(indices < (length + 1) // 2, indices, indices - length).astype(jnp.float32)
    return (2.0 * math.pi / length * signed) ** 2


def hartree_field(density):
    planes = density.shape[0]
    z_cosine, z_sine = dft_tables(NZ)
    y_cosine, y_sine = dft_tables(NY)
    x_cosine, x_sine = dft_tables(NX)
    forward_z = jnp.concatenate([z_cosine, -z_sine], axis=1)
    flattened = density.reshape(planes * NY, NZ)
    spectral = jnp.dot(
        flattened, forward_z, precision=lax.Precision.HIGHEST, preferred_element_type=jnp.float32
    )
    spectral = turn_axis(y_cosine, -y_sine, spectral.reshape(planes, NY, 2 * NZ), "ky,xyz->xkz")
    columns = lax.all_to_all(spectral, "space", split_axis=1, concat_axis=0, tiled=True)
    y_rows = columns.shape[1]
    spectral = turn_axis(x_cosine, -x_sine, columns, "kx,xyz->kyz")
    squares = (
        squared_waves(NX, 0, NX)[:, None, None]
        + squared_waves(NY, lax.axis_index("space") * y_rows, y_rows)[None, :, None]
        + squared_waves(NZ, 0, NZ)[None, None, :]
    )
    kernel = jnp.where(squares > 0, 4.0 * math.pi / jnp.where(squares > 0, squares, 1.0), 0.0)
    spectral = spectral * jnp.concatenate([kernel, kernel], axis=-1)
    spectral = turn_axis(x_cosine, x_sine, spectral, "kx,xyz->kyz")
    slabs = lax.all_to_all(spectral, "space", split_axis=0, concat_axis=1, tiled=True)
    spectral = turn_axis(y_cosine, y_sine, slabs, "ky,xyz->xkz")
    inverse_z = jnp.concatenate([z_cosine, -z_sine], axis=0)
    field_values = jnp.dot(
        spectral.reshape(planes * NY, 2 * NZ),
        inverse_z,
        precision=lax.Precision.HIGHEST,
        preferred_element_type=jnp.float32,
    )
    return (field_values / (NX * NY * NZ)).reshape(planes, NY * NZ)


def per_device(orbitals, potential, occupations):
    reach_cells = len(stencil_coeffs) - 1
    orbital_count = orbitals.shape[1]
    zero_copy = slab_rims(orbitals.astype(jnp.bfloat16), reach_cells)
    first_term = scaled_hamiltonian(orbitals, zero_copy, potential)
    first_copy = slab_rims(first_term.astype(jnp.bfloat16), reach_cells)
    second_term = 2.0 * scaled_hamiltonian(first_term, first_copy, potential) - orbitals
    prop_real = (
        bessel_terms[0] * orbitals[0]
        + 2.0 * bessel_terms[1] * first_term[1]
        - 2.0 * bessel_terms[2] * second_term[0]
    )
    prop_imag = (
        bessel_terms[0] * orbitals[1]
        - 2.0 * bessel_terms[1] * first_term[0]
        - 2.0 * bessel_terms[2] * second_term[1]
    )
    propagated = jnp.stack([prop_real, prop_imag])
    weights = occupations / (orbital_count * lax.axis_size("band"))
    partial_density = jnp.sum(
        weights[:, None, None] * (prop_real * prop_real + prop_imag * prop_imag), axis=0
    )
    density = over_pieces(partial_density, "band")
    hartree = hartree_field(density)
    return (propagated, density, hartree)


def solution(mesh):
    in_specs = (P(None, "band", "space", None), P("space", None), P("band"))
    out_specs = (P(None, "band", "space", None), P("space", None), P("space", None))
    return jax.shard_map(
        per_device, mesh=mesh, in_specs=in_specs, out_specs=out_specs, check_vma=False
    )
```

profile of v0, /device:TPU:1, one launch (start us, length us, event | category | flops | bytes accessed | tf_op | source)
XLA Modules:
  0.0 195.0 jit_solution(3471204599897894281)
XLA Ops:
  7.2 1.4 convert_element_type.63
  8.6 4.5 %collective-permute-start.1 = (bf16[2,4,3,9216]{3,1,2,0:T(4,128)(2,1)S(1)}, bf16[2,4,3,9216]{3,1,2,0:T(4,128)(2,1)S(1)}, u32[]{:S(2)}, u32[]{:S(2)}) collective-permute-start(bf16[2,4,3,9216]{3,1,2,0:T(4,128)(2,1)S(1)} %convert_element_type.63), channel_id=1, source_target_pairs={{0,1},{1,2},{2,3},{3,4},{4,5},{5,6},{6,7},{7,8},{8,9},{9,10},{10,1... | collective-permute-start | bytes 1327112 | tf_op jit(solution)/shard_map/ppermute | solution.py:22
  13.2 5.6 %collective-permute-start.2 = (bf16[2,4,3,9216]{3,1,2,0:T(4,128)(2,1)S(1)}, bf16[2,4,3,9216]{3,1,2,0:T(4,128)(2,1)S(1)}, u32[]{:S(2)}, u32[]{:S(2)}) collective-permute-start(bf16[2,4,3,9216]{3,1,2,0:T(4,128)(2,1)S(1)} %convert_element_type.63), channel_id=1, source_target_pairs={{1,0},{2,1},{3,2},{4,3},{5,4},{6,5},{7,6},{8,7},{9,8},{10,9},{11,1... | collective-permute-start | bytes 1327112 | tf_op jit(solution)/shard_map/ppermute | solution.py:22
  18.9 1.3 collective-permute-start
  20.2 1.3 collective-permute-start.3
  21.7 1.7 collective-permute-done
  23.5 0.2 constant_dynamic-update-slice_fusion.3
  23.7 0.2 constant_dynamic-update-slice_fusion.2
  23.9 0.2 constant_dynamic-update-slice_fusion.1
  24.0 3.6 %collective-permute-done.3 = bf16[2,4,1,9216]{3,1,2,0:T(4,128)(2,1)S(1)} collective-permute-done((bf16[2,4,1,9216]{3,1,2,0:T(4,128)(2,1)S(1)}, bf16[2,4,1,9216]{3,1,2,0:T(4,128)(2,1)S(1)}, u32[]{:S(2)}, u32[]{:S(2)}) %collective-permute-start.3) | collective-permute-done | bytes 147488 | tf_op jit(solution)/shard_map/ppermute | solution.py:22
  27.7 0.3 convert_element_type.64
  28.1 7.1 %broadcast_multiply_fusion = (f32[2,4,3,9216]{3,1,2,0:T(4,128)S(1)}, f32[2,4,3,9216]{3,1,2,0:T(4,128)S(1)}) fusion(f32[2,4,3,9216]{3,1,2,0:T(4,128)S(1)} %copy-done, f32[3,9216]{1,0:T(4,128)S(1)} %copy-done.2, pred[9216]{0:T(1024)(128)(4,1)S(1)} %get-tuple-element.20, pred[9216]{0:T(1024)(128)(4,1)S(1)} %get-tuple-element.21, ...), kind=kLoop, calls=%fused_computation.58 | loop fusion | flops 11280384 | bytes 10801152 | tf_op jit(solution)/shard_map/div | solution.py:60
  35.3 0.2 fusion.116
  35.6 1.4 collective-permute-start.4
  37.0 4.9 %collective-permute-start.5 = (bf16[2,4,3,9216]{3,1,2,0:T(4,128)(2,1)S(1)}, bf16[2,4,3,9216]{3,1,2,0:T(4,128)(2,1)S(1)}, u32[]{:S(2)}, u32[]{:S(2)}) collective-permute-start(bf16[2,4,3,9216]{3,1,2,0:T(4,128)(2,1)S(1)} %fusion.116), channel_id=1, source_target_pairs={{0,1},{1,2},{2,3},{3,4},{4,5},{5,6},{6,7},{7,8},{8,9},{9,10},{10,1... | collective-permute-start | bytes 1327112 | tf_op jit(solution)/shard_map/ppermute | solution.py:22
  42.0 1.9 collective-permute-start.6
  43.9 1.3 collective-permute-start.7
  45.3 1.9 collective-permute-done.5
  47.2 0.2 constant_dynamic-update-slice_fusion.8
  47.4 0.3 constant_dynamic-update-slice_fusion.7
  47.7 4.9 %collective-permute-done.6 = bf16[2,4,3,9216]{3,1,2,0:T(4,128)(2,1)S(1)} collective-permute-done((bf16[2,4,3,9216]{3,1,2,0:T(4,128)(2,1)S(1)}, bf16[2,4,3,9216]{3,1,2,0:T(4,128)(2,1)S(1)}, u32[]{:S(2)}, u32[]{:S(2)}) %collective-permute-start.6) | collective-permute-done | bytes 442400 | tf_op jit(solution)/shard_map/ppermute | solution.py:22
  52.5 0.2 constant_dynamic-update-slice_fusion.6
  52.7 1.4 collective-permute-done.7
  54.2 0.3 convert_element_type.66
  54.6 7.2 %multiply_subtract_fusion = f32[2,4,3,9216]{3,1,2,0:T(4,128)S(1)} fusion(f32[2,4,3,9216]{3,1,2,0:T(4,128)S(1)} %copy-done, f32[2,4,3,9216]{3,1,2,0:T(4,128)S(1)} %get-tuple-element.7, f32[2,4,3,9216]{3,1,2,0:T(4,128)S(1)} %slice.326, f32[2,4,11,9216]{3,1,2,0:T(4,128)S(1)} %convert_element_type.66, f32[3,9216]{1,0:T(4,128)S(1)} %broadcast_multiply_fusion.1, ...), kind=kLoop, calls=%fused_computation.46 | loop fusion | flops 11501568 | bytes 10801152 | tf_op jit(solution)/shard_map/sub | solution.py:143
  61.8 1.5 fusion.36
  63.3 0.2 fusion.62
  63.6 71.1 %all-gather.4.cloned.1.call-done = f32[16,3,9216]{2,1,0:T(4,128)} async-done(((f32[1,3,9216]{2,1,0:T(4,128)}), f32[16,3,9216]{2,1,0:T(4,128)}) %all-gather.4.cloned.1.call-update) | async-done | bytes 1769488 | tf_op jit(solution)/shard_map/all_gather | solution.py:26
  134.7 2.0 %reduce_sum.19 = f32[3,9216]{1,0:T(4,128)S(1)} reduce(f32[16,3,9216]{2,1,0:T(4,128)} %all-gather.4.cloned.1.call-done, f32[]{:T(128)} %constant.42.clone.1), dimensions={0}, to_apply=%region_1.2 | reduce | flops 414720 | bytes 1880068 | tf_op jit(solution)/shard_map/reduce_sum | solution.py:26
  136.9 0.6 fusion.41
  137.5 0.6 convolution_bitcast_fusion.2
  138.1 0.6 convolution_bitcast_fusion.3
  138.8 0.9 copy.20
  139.7 16.6 %all-to-all-start = ((f32[3,96,192]{2,0,1:T(4,128)}), f32[3,96,192]{2,0,1:T(4,128)S(1)}, u32[]{:S(2)}, u32[]{:S(2)}) async-start(f32[3,96,192]{2,0,1:T(4,128)} %copy.20), calls=%async_computation | async-start | bytes 786432 | tf_op jit(solution)/shard_map/all_to_all | solution.py:114
  156.4 10.0 %all-to-all-done = f32[3,96,192]{2,0,1:T(4,128)S(1)} async-done(((f32[3,96,192]{2,0,1:T(4,128)}), f32[3,96,192]{2,0,1:T(4,128)S(1)}, u32[]{:S(2)}, u32[]{:S(2)}) %all-to-all-start) | async-done | bytes 221216 | tf_op jit(solution)/shard_map/all_to_all | solution.py:114
  166.7 0.6 fusion.51
  167.3 0.6 fusion.56
  168.1 0.7 fusion.40
  168.8 0.7 fusion.39
  169.7 1.0 copy.23
  170.7 3.9 %all-to-all-start.1 = ((f32[96,3,192]{2,1,0:T(4,128)}), f32[96,3,192]{2,1,0:T(4,128)S(1)}, u32[]{:S(2)}, u32[]{:S(2)}) async-start(f32[96,3,192]{2,1,0:T(4,128)} %copy.23), calls=%async_computation.1 | async-start | bytes 786432 | tf_op jit(solution)/shard_map/all_to_all | solution.py:125
  174.6 1.1 pad_maximum_fusion
  175.7 9.2 %all-to-all-done.1 = f32[96,3,192]{2,1,0:T(4,128)S(1)} async-done(((f32[96,3,192]{2,1,0:T(4,128)}), f32[96,3,192]{2,1,0:T(4,128)S(1)}, u32[]{:S(2)}, u32[]{:S(2)}) %all-to-all-start.1) | async-done | bytes 221216 | tf_op jit(solution)/shard_map/all_to_all | solution.py:125
  185.1 0.8 convolution_bitcast_fusion
  185.9 0.8 convolution_bitcast_fusion.1
  186.8 0.2 copy.28
  186.9 0.4 convolution_multiply_fusion
  187.3 0.8 reshape.101
  (43 shorter events, 2.1 us)
Async XLA Ops:
  7.2 16.5 %copy-start = (f32[2,4,3,9216]{3,1,2,0:T(4,128)S(1)}, f32[2,4,3,9216]{3,1,2,0:T(4,128)}, u32[]{:S(2)}) copy-start(f32[2,4,3,9216]{3,1,2,0:T(4,128)} %param.3) | copy-start | bytes 2654212
  7.2 14.4 %copy-start.2 = (f32[3,9216]{1,0:T(4,128)S(1)}, f32[3,9216]{1,0:T(4,128)}, u32[]{:S(2)}) copy-start(f32[3,9216]{1,0:T(4,128)} %param.4) | copy-start | bytes 331780
  7.2 127.5 %all-gather.4.cloned.1.call-start = ((), (), s32[]{:S(2)}) async-start(), calls=%async_computation.2 | async-start | bytes 2506752 | tf_op jit(solution)/shard_map/all_gather | solution.py:26
  8.6 14.8 %collective-permute-start.1 = (bf16[2,4,3,9216]{3,1,2,0:T(4,128)(2,1)S(1)}, bf16[2,4,3,9216]{3,1,2,0:T(4,128)(2,1)S(1)}, u32[]{:S(2)}, u32[]{:S(2)}) collective-permute-start(bf16[2,4,3,9216]{3,1,2,0:T(4,128)(2,1)S(1)} %convert_element_type.63), channel_id=1, source_target_pairs={{0,1},{1,2},{2,3},{3,4},{4,5},{5,6},{6,7},{7,8},{8,9},{9,10},{10,1... | collective-permute-start | bytes 1327112 | tf_op jit(solution)/shard_map/ppermute | solution.py:22
  13.2 10.7 %collective-permute-start.2 = (bf16[2,4,3,9216]{3,1,2,0:T(4,128)(2,1)S(1)}, bf16[2,4,3,9216]{3,1,2,0:T(4,128)(2,1)S(1)}, u32[]{:S(2)}, u32[]{:S(2)}) collective-permute-start(bf16[2,4,3,9216]{3,1,2,0:T(4,128)(2,1)S(1)} %convert_element_type.63), channel_id=1, source_target_pairs={{1,0},{2,1},{3,2},{4,3},{5,4},{6,5},{7,6},{8,7},{9,8},{10,9},{11,1... | collective-permute-start | bytes 1327112 | tf_op jit(solution)/shard_map/ppermute | solution.py:22
  18.9 4.5 %collective-permute-start = (bf16[2,4,1,9216]{3,1,2,0:T(4,128)(2,1)S(1)}, bf16[2,4,1,9216]{3,1,2,0:T(4,128)(2,1)S(1)}, u32[]{:S(2)}, u32[]{:S(2)}) collective-permute-start(bf16[2,4,1,9216]{3,1,2,0:T(4,128)(2,1)S(1)} %get-tuple-element.19), channel_id=1, source_target_pairs={{0,2},{1,3},{2,4},{3,5},{4,6},{5,7},{6,8},{7,9},{8,10},{9,11},{10,... | collective-permute-start | bytes 442376 | tf_op jit(solution)/shard_map/ppermute | solution.py:22
  20.2 7.4 %collective-permute-start.3 = (bf16[2,4,1,9216]{3,1,2,0:T(4,128)(2,1)S(1)}, bf16[2,4,1,9216]{3,1,2,0:T(4,128)(2,1)S(1)}, u32[]{:S(2)}, u32[]{:S(2)}) collective-permute-start(bf16[2,4,1,9216]{3,1,2,0:T(4,128)(2,1)S(1)} %get-tuple-element.18), channel_id=1, source_target_pairs={{2,0},{3,1},{4,2},{5,3},{6,4},{7,5},{8,6},{9,7},{10,8},{11,9},{12,... | collective-permute-start | bytes 442376 | tf_op jit(solution)/shard_map/ppermute | solution.py:22
  35.3 1.8 copy-start.3
  35.6 9.6 %collective-permute-start.4 = (bf16[2,4,1,9216]{3,1,2,0:T(4,128)(2,1)S(1)}, bf16[2,4,1,9216]{3,1,2,0:T(4,128)(2,1)S(1)}, u32[]{:S(2)}, u32[]{:S(2)}) collective-permute-start(bf16[2,4,1,9216]{3,1,2,0:T(4,128)(2,1)S(1)} %get-tuple-element.17), channel_id=1, source_target_pairs={{0,2},{1,3},{2,4},{3,5},{4,6},{5,7},{6,8},{7,9},{8,10},{9,11},{10,... | collective-permute-start | bytes 442376 | tf_op jit(solution)/shard_map/ppermute | solution.py:22
  37.0 10.2 %collective-permute-start.5 = (bf16[2,4,3,9216]{3,1,2,0:T(4,128)(2,1)S(1)}, bf16[2,4,3,9216]{3,1,2,0:T(4,128)(2,1)S(1)}, u32[]{:S(2)}, u32[]{:S(2)}) collective-permute-start(bf16[2,4,3,9216]{3,1,2,0:T(4,128)(2,1)S(1)} %fusion.116), channel_id=1, source_target_pairs={{0,1},{1,2},{2,3},{3,4},{4,5},{5,6},{6,7},{7,8},{8,9},{9,10},{10,1... | collective-permute-start | bytes 1327112 | tf_op jit(solution)/shard_map/ppermute | solution.py:22
  42.0 10.5 %collective-permute-start.6 = (bf16[2,4,3,9216]{3,1,2,0:T(4,128)(2,1)S(1)}, bf16[2,4,3,9216]{3,1,2,0:T(4,128)(2,1)S(1)}, u32[]{:S(2)}, u32[]{:S(2)}) collective-permute-start(bf16[2,4,3,9216]{3,1,2,0:T(4,128)(2,1)S(1)} %fusion.116), channel_id=1, source_target_pairs={{1,0},{2,1},{3,2},{4,3},{5,4},{6,5},{7,6},{8,7},{9,8},{10,9},{11,1... | collective-permute-start | bytes 1327112 | tf_op jit(solution)/shard_map/ppermute | solution.py:22
  43.9 10.2 %collective-permute-start.7 = (bf16[2,4,1,9216]{3,1,2,0:T(4,128)(2,1)S(1)}, bf16[2,4,1,9216]{3,1,2,0:T(4,128)(2,1)S(1)}, u32[]{:S(2)}, u32[]{:S(2)}) collective-permute-start(bf16[2,4,1,9216]{3,1,2,0:T(4,128)(2,1)S(1)} %get-tuple-element.16), channel_id=1, source_target_pairs={{2,0},{3,1},{4,2},{5,3},{6,4},{7,5},{8,6},{9,7},{10,8},{11,9},{12,... | collective-permute-start | bytes 442376 | tf_op jit(solution)/shard_map/ppermute | solution.py:22
  136.8 2.0 %copy-start.1 = (f32[3,9216]{1,0:T(4,128)}, f32[3,9216]{1,0:T(4,128)S(1)}, u32[]{:S(2)}) copy-start(f32[3,9216]{1,0:T(4,128)S(1)} %reduce_sum.19) | copy-start | bytes 331780
  139.7 26.7 %all-to-all-start = ((f32[3,96,192]{2,0,1:T(4,128)}), f32[3,96,192]{2,0,1:T(4,128)S(1)}, u32[]{:S(2)}, u32[]{:S(2)}) async-start(f32[3,96,192]{2,0,1:T(4,128)} %copy.20), calls=%async_computation | async-start | bytes 786432 | tf_op jit(solution)/shard_map/all_to_all | solution.py:114
  170.7 14.2 %all-to-all-start.1 = ((f32[96,3,192]{2,1,0:T(4,128)}), f32[96,3,192]{2,1,0:T(4,128)S(1)}, u32[]{:S(2)}, u32[]{:S(2)}) async-start(f32[96,3,192]{2,1,0:T(4,128)} %copy.23), calls=%async_computation.1 | async-start | bytes 786432 | tf_op jit(solution)/shard_map/all_to_all | solution.py:125
Sparse Core Ops, SparseCore 0:
  63.4 71.2 all-gather.3
where the time goes:
time: 196 us; the launch traced here: 195 us
  waiting for transfers between devices  104 us (53%)
  starting transfers between devices  42.7 us (22%)
  other arithmetic  22.8 us (12%)
  between operations  14.5 us (7%)
  matrix products  6.34 us (3%)
  local copies, waits for them, and re-layouts  4.79 us (2%)
    all_gather x1, waiting for transfers between devices, over_pieces(): return lax.all_gather(x, axis).sum(0)  71.1 us
    ppermute x8, starting transfers between devices, from_behind(): return lax.ppermute(x, axis, pairs)  22.3 us
    all_to_all x1, starting transfers between devices, hartree_field(): lax.all_to_all(spectral, 'space', split_axis=1, concat_axis=0, tiled=True)  16.6 us
    ppermute x8, waiting for transfers between devices, from_behind(): return lax.ppermute(x, axis, pairs)  13.5 us
    all_to_all x1, waiting for transfers between devices, hartree_field(): lax.all_to_all(spectral, 'space', split_axis=1, concat_axis=0, tiled=True)  10 us
    all_to_all x1, waiting for transfers between devices, hartree_field(): lax.all_to_all(spectral, 'space', split_axis=0, concat_axis=1, tiled=True)  9.18 us
    sub x1, other arithmetic, per_device(): 2.0 * scaled_hamiltonian(first_term, first_copy, potential) - orbitals  7.16 us
    div x1, other arithmetic, scaled_hamiltonian(): return (energy - energy_shift * center) / energy_scale  7.12 us
  transfers between devices with their start and end apart: 11, of which 8 were waited for; matrix products, arithmetic and copies ran while one was open for 2% of the time, Pallas kernels for 0%

commit v1 on v0

v1 whole, which is shorter than its diff:
```python
import functools
import math

import jax
import jax.numpy as jnp
import ml_dtypes
import numpy as np
from jax import lax
from jax.experimental import pallas as pl
from jax.experimental.pallas import tpu as pltpu
from jax.sharding import PartitionSpec as P

NX = 96
NY = 96
NZ = 96

stencil_coeffs = (-205.0 / 72.0, 8.0 / 5.0, -1.0 / 5.0, 8.0 / 315.0, -1.0 / 560.0)
energy_shift = 6.0
energy_scale = 8.0
bessel_terms = (0.7651976865579666, 0.44005058574493355, 0.11490348493190049)
scaled_coeffs = tuple(c / stencil_coeffs[1] for c in stencil_coeffs)

MESH = pl.DeviceIdType.MESH
PLANES = 3
FIELDS = 8
CELLS = NY * NZ
FOLD = CELLS // 2
BLOCK = 4 * NZ
BLOCKS = CELLS // BLOCK
CHUNKS = 4
CHUNK = FOLD // CHUNKS
PER_CHUNK = CHUNK // BLOCK
WINDOW = 3 * BLOCK
PADDED = FOLD + 2 * BLOCK
SPACE = 32
BAND = 16
OWNERS = 9
ORBITALS = 64


def band_matrix():
    table = np.zeros((WINDOW, BLOCK))
    for cell in range(BLOCK):
        z = cell % NZ
        for offset in range(1, 5):
            c = scaled_coeffs[offset]
            table[BLOCK + cell + offset * NZ, cell] += c
            table[BLOCK + cell - offset * NZ, cell] += c
            if z + offset < NZ:
                table[BLOCK + cell + offset, cell] += c
            if z - offset >= 0:
                table[BLOCK + cell - offset, cell] += c
    return table.astype(ml_dtypes.bfloat16)


def real_basis(length):
    cells = np.arange(length)
    rows = [np.full(length, 1.0 / math.sqrt(length))]
    waves = [0]
    for k in range(1, length // 2):
        phase = 2.0 * math.pi * ((k * cells) % length) / length
        rows.append(math.sqrt(2.0 / length) * np.cos(phase))
        rows.append(math.sqrt(2.0 / length) * np.sin(phase))
        waves += [k, k]
    rows.append(np.where(cells % 2 == 0, 1.0, -1.0) / math.sqrt(length))
    waves.append(length // 2)
    return np.stack(rows), (2.0 * math.pi / length * np.array(waves)) ** 2


def transform_tables():
    basis, squares = real_basis(NY)
    order = np.array([4 * block + r for r in range(4) for block in range(BLOCKS)])
    forward_y = basis[:, order]
    lanes = np.arange(128)
    spread = np.stack([basis[lanes % 64], basis[64 + lanes % 32]])
    forward_z = np.zeros((4, NZ, 4, 2, 128))
    for r in range(4):
        forward_z[r, :, r] = np.transpose(spread, (2, 0, 1))
    forward_z = forward_z.reshape(BLOCK, 1024)
    row = np.arange(72)[:, None]
    mode_y = np.where(row < 48, row + 48 * (lanes >= 64), row - 48 + 24 * (lanes // 32))
    mode_z = np.where(row < 48, lanes % 64, 64 + lanes % 32)
    across = squares[mode_y] + squares[mode_z]
    cells = np.arange(NX)
    signed = np.where(cells < NX // 2, cells, cells - NX)
    along = (2.0 * math.pi / NX * signed) ** 2
    total = along[:, None, None] + across
    kernel = np.where(total > 0, 4.0 * math.pi / np.where(total > 0, total, 1.0), 0.0)
    green = np.real(np.fft.ifft(kernel, axis=0))
    green = green[(np.arange(NX + 2) - 2) % NX]
    green = green.reshape(NX + 2, OWNERS, 8, 128).transpose(1, 0, 2, 3)
    f32 = np.float32
    return (
        forward_z.astype(f32),
        forward_y.astype(f32),
        forward_y.T.copy().astype(f32),
        forward_z.T.copy().astype(f32),
        green.astype(f32),
    )


def exact_dot(a, b):
    return lax.dot_general(
        a,
        b,
        (((1,), (0,)), ((), ())),
        precision=lax.Precision.HIGHEST,
        preferred_element_type=jnp.float32,
    )


def body(
    orb_hbm, pot_ref, occ_ref, band_hbm, fz_hbm, fy_hbm, iy_hbm, iz_hbm, green_hbm,
    prop_hbm, dens_ref, hart_ref,
    field, first, prop, own0, own1, rim0, rim1, lines,
    band_ref, fz_ref, fy_ref, iy_ref, iz_ref, green_ref,
    modes, shares, summed, layer, answer, dens_modes, hart_modes,
    load_sem, table_sem, store_sem, halo_send, halo_recv,
    share_send, share_recv, layer_send, layer_recv, dens_send, dens_recv, hart_send, hart_recv,
):
    s = lax.axis_index("space")
    z = lax.axis_index("band")
    core = lax.rem(s, 2)
    f32 = jnp.float32
    bf16 = jnp.bfloat16

    loads = [
        pltpu.make_async_copy(orb_hbm.at[part], field.at[:, pl.ds(4 * part, 4), :], load_sem.at[part])
        for part in range(2)
    ]
    for copy in loads:
        copy.start()
    owner = (OWNERS * z + BAND - 1) // BAND
    owner_index = jnp.minimum(owner, OWNERS - 1)
    is_owner = (BAND * owner) // OWNERS == z
    tables = [
        pltpu.make_async_copy(src, dst, table_sem.at[i])
        for i, (src, dst) in enumerate(
            [
                (band_hbm, band_ref),
                (fz_hbm, fz_ref),
                (fy_hbm, fy_ref),
                (iy_hbm, iy_ref),
                (iz_hbm, iz_ref),
                (green_hbm.at[owner_index], green_ref),
            ]
        )
    ]
    for copy in tables:
        copy.start()

    barrier = pltpu.get_barrier_semaphore()

    def greet_space(k, carry):
        pl.semaphore_signal(
            barrier, inc=1, device_id={"space": lax.rem(s + k, SPACE)}, device_id_type=MESH
        )
        return carry

    def greet_band(k, carry):
        pl.semaphore_signal(
            barrier, inc=1, device_id={"band": lax.rem(z + k, BAND)}, device_id_type=MESH
        )
        return carry

    lax.fori_loop(1, BAND, greet_band, 0)
    lax.fori_loop(1, SPACE, greet_space, 0)

    def lanes_of(c, extra=0, size=CHUNK):
        return pl.ds(pl.multiple_of(c * CHUNK + extra, 128), size)

    outward = 2 * core - 1
    owns = (own0, own1)
    rims = (rim0, rim1)

    def halo(phase, kind, c):
        own, rim = owns[phase], rims[phase]
        inside = lanes_of(c, BLOCK)
        outside = lanes_of(c)
        if kind == 0:
            src = own.at[:, :, inside]
            dst = rim.at[1 - core, pl.ds(core, 3), :, outside]
            step = outward
        elif kind == 1:
            src = own.at[:, :, inside]
            dst = rim.at[core, pl.ds(1 - core, 3), :, outside]
            step = -outward
        elif kind == 2:
            src = own.at[2 * (1 - core), :, inside]
            dst = rim.at[core, 3 * core, :, outside]
            step = -2 * outward
        else:
            src = rim.at[core, 3 * (1 - core), :, outside]
            dst = rim.at[core, 3 * core, :, outside]
            step = -outward
        return pltpu.make_async_remote_copy(
            src_ref=src,
            dst_ref=dst,
            send_sem=halo_send.at[phase, kind, c],
            recv_sem=halo_recv.at[phase, kind, c],
            device_id={"space": lax.rem(s + step + SPACE, SPACE)},
            device_id_type=MESH,
        )

    def fold_edges(source, own):
        zeros = jnp.zeros((FIELDS, BLOCK), f32)
        for p in range(PLANES):
            own[p, :, 0:BLOCK] = jnp.concatenate(
                [zeros, source[p, :, FOLD - BLOCK : FOLD]], axis=0
            ).astype(bf16)
            own[p, :, PADDED - BLOCK : PADDED] = jnp.concatenate(
                [source[p, :, FOLD : FOLD + BLOCK], zeros], axis=0
            ).astype(bf16)

    for copy in loads:
        copy.wait()
    pl.semaphore_wait(barrier, SPACE + BAND - 2)

    def ship(c, carry):
        for p in range(PLANES):
            own0[p, :, lanes_of(c, BLOCK)] = jnp.concatenate(
                [field[p, :, lanes_of(c)], field[p, :, lanes_of(c, FOLD)]], axis=0
            ).astype(bf16)
        for kind in range(3):
            halo(0, kind, c).start()
        return carry

    lax.fori_loop(0, CHUNKS, ship, 0)
    fold_edges(field, own0)
    tables[0].wait()

    near_left = jnp.where(s >= 1, 1.0, 0.0).astype(f32)
    far_left = jnp.where(s >= 2, 1.0, 0.0).astype(f32)
    near_right = jnp.where(s <= SPACE - 2, 1.0, 0.0).astype(f32)
    far_right = jnp.where(s <= SPACE - 3, 1.0, 0.0).astype(f32)
    left_weights = (far_left, near_left, near_left, near_left)
    right_weights = (near_right, near_right, near_right, far_right)

    gain = stencil_coeffs[1] / (2.0 * energy_scale)
    level = -(energy_shift + 1.5 * stencil_coeffs[0]) / energy_scale

    def arrive(phase, c):
        halo(phase, 0, c).wait_recv()
        halo(phase, 3, c).start()
        for kind in (1, 2, 3):
            halo(phase, kind, c).wait_recv()

    def stencil(phase, source, c, finish):
        own, rim = owns[phase], rims[phase]
        windows = [
            own[p, :, lanes_of(c, b * BLOCK, WINDOW)]
            for p in range(PLANES)
            for b in range(PER_CHUNK)
        ]
        flat = jnp.dot(
            jnp.concatenate(windows, axis=0), band_ref[...], preferred_element_type=f32
        )
        for b in range(PER_CHUNK):
            outside = lanes_of(c, b * BLOCK, BLOCK)
            inside = lanes_of(c, (b + 1) * BLOCK, BLOCK)
            stack = [rim[0, k, :, outside].astype(f32) * left_weights[k] for k in range(4)]
            stack += [own[p, :, inside].astype(f32) for p in range(PLANES)]
            stack += [rim[1, k, :, outside].astype(f32) * right_weights[k] for k in range(4)]
            for p in range(PLANES):
                across = stack[p + 5] + stack[p + 3]
                for offset in range(2, 5):
                    across = across + scaled_coeffs[offset] * (
                        stack[p + 4 + offset] + stack[p + 4 - offset]
                    )
                at = 16 * (p * PER_CHUNK + b)
                across = gain * (across + flat[at : at + 16])
                for half in range(2):
                    lanes = lanes_of(c, half * FOLD + b * BLOCK, BLOCK)
                    centre = source[p, :, lanes]
                    factor = pot_ref[p : p + 1, lanes] * (1.0 / energy_scale) + level
                    value = centre * factor - across[8 * half : 8 * half + 8]
                    finish(p, b, half, lanes, centre, value)

    def first_chunk(c, carry):
        arrive(0, c)
        values = {}

        def finish(p, b, half, lanes, centre, value):
            first[p, :, lanes] = value
            values[p, b, half] = value
            if half == 1:
                own1[p, :, lanes_of(c, (b + 1) * BLOCK, BLOCK)] = jnp.concatenate(
                    [values[p, b, 0], value], axis=0
                ).astype(bf16)

        stencil(0, field, c, finish)
        for kind in range(3):
            halo(1, kind, c).start()
        return carry

    lax.fori_loop(0, CHUNKS, first_chunk, 0)
    fold_edges(first, own1)

    rows = lax.broadcasted_iota(jnp.int32, (FIELDS, BLOCK), 0)
    weight = jnp.zeros((FIELDS, BLOCK), f32)
    for o in range(4):
        weight = jnp.where(lax.rem(rows, 4) == o, occ_ref[o] * (1.0 / ORBITALS), weight)
    sign = jnp.where(rows < 4, 2.0 * bessel_terms[1], -2.0 * bessel_terms[1]).astype(f32)

    def stores(c, half, part):
        lanes = lanes_of(c, half * FOLD)
        return pltpu.make_async_copy(
            prop.at[:, pl.ds(4 * part, 4), lanes],
            prop_hbm.at[part, :, :, lanes],
            store_sem.at[c, half, part],
        )

    def second_chunk(c, carry):
        arrive(1, c)

        def finish(p, b, half, lanes, centre, value):
            swapped = jnp.concatenate([centre[4:8], centre[0:4]], axis=0)
            result = (
                (bessel_terms[0] + 2.0 * bessel_terms[2]) * field[p, :, lanes]
                + sign * swapped
                - (4.0 * bessel_terms[2]) * value
            )
            prop[p, :, lanes] = result
            share = jnp.sum(weight * (result * result), axis=0, keepdims=True)
            lines[pl.ds(p * BLOCKS + half * (BLOCKS // 2) + c * PER_CHUNK + b, 1), :] = share

        stencil(1, first, c, finish)
        for half in range(2):
            for part in range(2):
                stores(c, half, part).start()
        return carry

    lax.fori_loop(0, CHUNKS, second_chunk, 0)

    for copy in tables[1:]:
        copy.wait()
    turned = exact_dot(lines[...], fz_ref[...])
    stacked = jnp.concatenate(
        [
            jnp.concatenate(
                [
                    turned[p * BLOCKS : (p + 1) * BLOCKS, r * 256 : (r + 1) * 256]
                    for r in range(4)
                ],
                axis=0,
            )
            for p in range(PLANES)
        ],
        axis=1,
    )
    spectral = exact_dot(fy_ref[...], stacked)
    lane = lax.broadcasted_iota(jnp.int32, (1, 128), 1)
    for p in range(PLANES):
        wide = spectral[:, p * 256 : p * 256 + 128]
        tail = spectral[:, p * 256 + 128 : (p + 1) * 256]
        head = jnp.where(lane < 64, wide[0:48], wide[48:96])
        rest = tail[0:24]
        for quarter in range(1, 4):
            rest = jnp.where(lane >= 32 * quarter, tail[24 * quarter : 24 * quarter + 24], rest)
        for o in range(6):
            modes[o, p] = head[8 * o : 8 * o + 8]
        for o in range(3):
            modes[6 + o, p] = rest[8 * o : 8 * o + 8]

    def share_copy(o, source):
        return pltpu.make_async_remote_copy(
            src_ref=modes.at[o],
            dst_ref=shares.at[source],
            send_sem=share_send.at[o],
            recv_sem=share_recv.at[source],
            device_id={"band": (BAND * o) // OWNERS},
            device_id_type=MESH,
        )

    for o in range(OWNERS):
        @pl.when((BAND * o) // OWNERS != z)
        def _():
            share_copy(o, z).start()

    def layer_copy(k):
        return pltpu.make_async_remote_copy(
            src_ref=summed,
            dst_ref=layer.at[SPACE - k],
            send_sem=layer_send.at[k],
            recv_sem=layer_recv.at[SPACE - k],
            device_id={"space": lax.rem(s + k, SPACE)},
            device_id_type=MESH,
        )

    def band_copy(src, dst, send, recv, k):
        return pltpu.make_async_remote_copy(
            src_ref=src,
            dst_ref=dst.at[owner_index],
            send_sem=send.at[k],
            recv_sem=recv.at[owner_index],
            device_id={"band": lax.rem(z + k, BAND)},
            device_id_type=MESH,
        )

    @pl.when(is_owner)
    def _():
        def collect(k, total):
            source = lax.rem(z + k, BAND)
            pltpu.make_async_copy(modes.at[0], shares.at[source], share_recv.at[source]).wait()
            return total + shares[source]

        total = lax.fori_loop(1, BAND, collect, modes[owner_index])
        summed[...] = total
        layer[0] = total
        dens_modes[owner_index] = total

        def out_layer(k, carry):
            layer_copy(k).start()
            return carry

        lax.fori_loop(1, SPACE, out_layer, 0)

        def out_dens(k, carry):
            band_copy(summed, dens_modes, dens_send, dens_recv, k).start()
            return carry

        lax.fori_loop(1, BAND, out_dens, 0)

        def apply(r, total):
            out = list(total)
            for q in range(PLANES):
                value = layer[r, q]
                for p in range(PLANES):
                    out[p] = out[p] + green_ref[3 * r + q - p + 2] * value
            return tuple(out)

        def collect_layer(r, total):
            pltpu.make_async_copy(summed, layer.at[r], layer_recv.at[r]).wait()
            return apply(r, total)

        zero = jnp.zeros((8, 128), f32)
        result = lax.fori_loop(1, SPACE, collect_layer, apply(0, (zero, zero, zero)))
        for p in range(PLANES):
            answer[p] = result[p]
            hart_modes[owner_index, p] = result[p]

        def out_hart(k, carry):
            band_copy(answer, hart_modes, hart_send, hart_recv, k).start()
            return carry

        lax.fori_loop(1, BAND, out_hart, 0)

    def back(spec_ref):
        pieces = []
        for p in range(PLANES):
            head = jnp.concatenate([spec_ref[o, p] for o in range(6)], axis=0)
            rest = jnp.concatenate([spec_ref[6 + o, p] for o in range(3)], axis=0)
            upper = jnp.concatenate(
                [jnp.where(lane < 64, head, 0.0), jnp.where(lane >= 64, head, 0.0)], axis=0
            )
            lower = jnp.concatenate(
                [jnp.where(lane // 32 == quarter, rest, 0.0) for quarter in range(4)], axis=0
            )
            pieces += [upper, lower]
        rows_y = exact_dot(iy_ref[...], jnp.concatenate(pieces, axis=1))
        flat = jnp.concatenate(
            [
                jnp.concatenate(
                    [
                        rows_y[r * BLOCKS : (r + 1) * BLOCKS, p * 256 : (p + 1) * 256]
                        for r in range(4)
                    ],
                    axis=1,
                )
                for p in range(PLANES)
            ],
            axis=0,
        )
        return exact_dot(flat, iz_ref[...])

    def put(out_ref, values):
        for p in range(PLANES):
            for block in range(BLOCKS):
                at = p * BLOCKS + block
                out_ref[p : p + 1, block * BLOCK : (block + 1) * BLOCK] = values[at : at + 1]

    def gathered(dst, recv):
        for o in range(OWNERS):
            @pl.when((BAND * o) // OWNERS != z)
            def _():
                pltpu.make_async_copy(summed, dst.at[o], recv.at[o]).wait()

    gathered(dens_modes, dens_recv)
    put(dens_ref, back(dens_modes))
    gathered(hart_modes, hart_recv)
    put(hart_ref, back(hart_modes))

    @pl.when(is_owner)
    def _():
        def drain_layer(k, carry):
            layer_copy(k).wait_send()
            return carry

        lax.fori_loop(1, SPACE, drain_layer, 0)

        def drain_band(k, carry):
            band_copy(summed, dens_modes, dens_send, dens_recv, k).wait_send()
            band_copy(answer, hart_modes, hart_send, hart_recv, k).wait_send()
            return carry

        lax.fori_loop(1, BAND, drain_band, 0)

    for o in range(OWNERS):
        @pl.when((BAND * o) // OWNERS != z)
        def _():
            share_copy(o, z).wait_send()

    def drain(c, carry):
        for phase in range(2):
            for kind in range(4):
                halo(phase, kind, c).wait_send()
        for half in range(2):
            for part in range(2):
                stores(c, half, part).wait()
        return carry

    lax.fori_loop(0, CHUNKS, drain, 0)


def per_device(orbitals, potential, occupations):
    f32 = jnp.float32
    bf16 = jnp.bfloat16
    forward_z, forward_y, inverse_y, inverse_z, green = transform_tables()
    vmem = pltpu.VMEM
    dma = pltpu.SemaphoreType.DMA
    anywhere = pl.BlockSpec(memory_space=pl.ANY)
    whole = pl.BlockSpec(memory_space=pltpu.VMEM)
    prop, dens, hart = pl.pallas_call(
        body,
        out_shape=(
            jax.ShapeDtypeStruct((2, PLANES, 4, CELLS), f32),
            jax.ShapeDtypeStruct((PLANES, CELLS), f32),
            jax.ShapeDtypeStruct((PLANES, CELLS), f32),
        ),
        in_specs=[anywhere, whole, pl.BlockSpec(memory_space=pltpu.SMEM)] + [anywhere] * 6,
        out_specs=(anywhere, whole, whole),
        scratch_shapes=[
            vmem((PLANES, FIELDS, CELLS), f32),
            vmem((PLANES, FIELDS, CELLS), f32),
            vmem((PLANES, FIELDS, CELLS), f32),
            vmem((PLANES, 16, PADDED), bf16),
            vmem((PLANES, 16, PADDED), bf16),
            vmem((2, 4, 16, FOLD), bf16),
            vmem((2, 4, 16, FOLD), bf16),
            vmem((PLANES * BLOCKS, BLOCK), f32),
            vmem((WINDOW, BLOCK), bf16),
            vmem((BLOCK, 1024), f32),
            vmem((NY, NY), f32),
            vmem((NY, NY), f32),
            vmem((1024, BLOCK), f32),
            vmem((NX + 2, 8, 128), f32),
            vmem((OWNERS, PLANES, 8, 128), f32),
            vmem((BAND, PLANES, 8, 128), f32),
            vmem((PLANES, 8, 128), f32),
            vmem((SPACE, PLANES, 8, 128), f32),
            vmem((PLANES, 8, 128), f32),
            vmem((OWNERS, PLANES, 8, 128), f32),
            vmem((OWNERS, PLANES, 8, 128), f32),
            dma((2,)),
            dma((6,)),
            dma((CHUNKS, 2, 2)),
            dma((2, 4, CHUNKS)),
            dma((2, 4, CHUNKS)),
            dma((OWNERS,)),
            dma((BAND,)),
            dma((SPACE,)),
            dma((SPACE,)),
            dma((BAND,)),
            dma((OWNERS,)),
            dma((BAND,)),
            dma((OWNERS,)),
        ],
        compiler_params=pltpu.CompilerParams(
            collective_id=0, has_side_effects=True, vmem_limit_bytes=40 * 2**20
        ),
    )(
        jnp.transpose(orbitals, (0, 2, 1, 3)),
        potential,
        occupations,
        jnp.asarray(band_matrix()),
        jnp.asarray(forward_z),
        jnp.asarray(forward_y),
        jnp.asarray(inverse_y),
        jnp.asarray(inverse_z),
        jnp.asarray(green),
    )
    return jnp.transpose(prop, (0, 2, 1, 3)), dens, hart


def solution(mesh):
    in_specs = (P(None, "band", "space", None), P("space", None), P("band"))
    out_specs = (P(None, "band", "space", None), P("space", None), P("space", None))
    return jax.shard_map(
        per_device, mesh=mesh, in_specs=in_specs, out_specs=out_specs, check_vma=False
    )
```

time: 196 us -> 82.4 us (0.42)
  waiting for transfers between devices: 104 us -> 0 us
  Pallas kernels: 0 us -> 68.7 us
  starting transfers between devices: 42.7 us -> 0 us
  other arithmetic: 22.8 us -> 0 us
  between operations: 14.5 us -> 0.66 us
  local copies, waits for them, and re-layouts: 4.79 us -> 12.6 us
  matrix products: 6.34 us -> 0 us
    all_gather x1 -> x0, waiting for transfers between devices: 71.1 us -> none  [over_pieces(): return lax.all_gather(x, axis).sum(0)]
    pallas_call x0 -> x1, Pallas kernels: none -> 68.7 us  [per_device(): pl.pallas_call(body, out_shape=(jax.ShapeDtypeStruct((2, PLANES, 4, CELLS...]
    ppermute x8 -> x0, starting transfers between devices: 22.3 us -> none  [from_behind(): return lax.ppermute(x, axis, pairs)]
    all_to_all x2 -> x0, starting transfers between devices: 20.5 us -> none  [the longest x1 16.6 us: hartree_field(): lax.all_to_all(spectral, 'space', split_axis=1, concat_axis=0, tiled=True)]
    all_to_all x2 -> x0, waiting for transfers between devices: 19.2 us -> none  [the longest x1 10 us: hartree_field(): lax.all_to_all(spectral, 'space', split_axis=1, concat_axis=0, tiled=True)]
    ppermute x8 -> x0, waiting for transfers between devices: 13.5 us -> none  [from_behind(): return lax.ppermute(x, axis, pairs)]
    unnamed x14 -> x21, local copies, waits for them, and re-layouts: 0.86 us -> 12.6 us
    sub x5 -> x0, other arithmetic: 7.51 us -> none  [the longest x1 7.16 us: per_device(): 2.0 * scaled_hamiltonian(first_term, first_copy, potential) - orbitals]
  transfers between devices with their start and end apart: 11 -> 0, of which waited for: 8 -> 0; matrix products, arithmetic and copies ran while one was open for 2% -> 0% of each run, Pallas kernels for 0% -> 0%
where the time goes in v1:
time: 82.4 us; the launch traced here: 81.9 us
  Pallas kernels  68.7 us (83%)
  local copies, waits for them, and re-layouts  12.6 us (15%)
    pallas_call x1, Pallas kernels, per_device(): pl.pallas_call(body, out_shape=(jax.ShapeDtypeStruct((2, PLANES, 4, CELLS...  68.7 us
    unnamed x21, local copies, waits for them, and re-layouts  12.6 us

profile of v1, /device:TPU:1, one launch (start us, length us, event | category | flops | bytes accessed | tf_op | source)
XLA Modules:
  0.0 81.9 jit_solution(405381050899297824)
XLA Ops:
  0.6 0.0 copy-start
  0.6 2.0 %copy-done = f32[9,98,8,128]{3,2,1,0:T(8,128)S(1)} copy-done((f32[9,98,8,128]{3,2,1,0:T(8,128)S(1)}, f32[9,98,8,128]{3,2,1,0:T(8,128)}, u32[]{:S(2)}) %copy-start) | copy-done | bytes 3612696
  2.7 0.0 copy-start.1
  2.7 1.4 %copy-done.1 = f32[1024,384]{1,0:T(8,128)S(1)} copy-done((f32[1024,384]{1,0:T(8,128)S(1)}, f32[1024,384]{1,0:T(8,128)}, u32[]{:S(2)}) %copy-start.1) | copy-done | bytes 1572888
  4.1 0.0 copy-start.2
  4.1 1.4 %copy-done.2 = f32[384,1024]{1,0:T(8,128)S(1)} copy-done((f32[384,1024]{1,0:T(8,128)S(1)}, f32[384,1024]{1,0:T(8,128)}, u32[]{:S(2)}) %copy-start.2) | copy-done | bytes 1572888
  5.5 0.0 copy-start.3
  5.5 1.2 %copy-done.3 = f32[2,4,3,9216]{3,1,2,0:T(4,128)S(1)} copy-done((f32[2,4,3,9216]{3,1,2,0:T(4,128)S(1)}, f32[2,4,3,9216]{3,1,2,0:T(4,128)}, u32[]{:S(2)}) %copy-start.3) | copy-done | bytes 884760
  6.6 0.0 copy-start.4
  6.6 1.2 %copy-done.4 = bf16[1152,384]{1,0:T(8,128)(2,1)S(1)} copy-done((bf16[1152,384]{1,0:T(8,128)(2,1)S(1)}, bf16[1152,384]{1,0:T(8,128)(2,1)}, u32[]{:S(2)}) %copy-start.4) | copy-done | bytes 884760
  7.8 0.0 copy-start.5
  7.8 0.9 %copy-done.5 = f32[3,9216]{1,0:T(4,128)S(1)} copy-done((f32[3,9216]{1,0:T(4,128)S(1)}, f32[3,9216]{1,0:T(4,128)}, u32[]{:S(2)}) %copy-start.5) | copy-done | bytes 110616
  8.7 0.0 copy-start.6
  8.7 0.8 copy-done.6
  9.5 0.0 copy-start.7
  9.5 0.8 copy-done.7
  10.3 0.0 copy-start.8
  10.3 0.7 copy-done.8
  11.0 68.7 %shard_map.112 = (f32[2,3,4,9216]{3,2,1,0:T(4,128)S(1)}, f32[3,9216]{1,0:T(4,128)S(1)}, f32[3,9216]{1,0:T(4,128)S(1)}) custom-call(f32[2,3,4,9216]{3,2,1,0:T(4,128)S(1)} %bitcast.2, f32[3,9216]{1,0:T(4,128)S(1)} %copy-done.5, f32[4]{0:T(128)S(1)} %copy-done.8, bf16[1152,384]{1,0:T(8,128)(2,1)S(1)} %copy-done.4, f32[384,1024]{1,0:T(8,128)S(1)} %copy-done.2, ...), custom_call_target="tpu_custom_call" | custom-call | tf_op jit(solution)/shard_map/pallas_call | solution.py:533
  79.7 0.9 %copy.15 = f32[2,4,3,9216]{3,1,2,0:T(4,128)} copy(f32[2,4,3,9216]{3,1,2,0:T(4,128)S(1)} %bitcast.3) | data formatting | bytes 1769472
  80.6 0.7 copy.16
  81.3 0.7 copy.17
Async XLA Ops:
  0.6 2.0 %copy-start = (f32[9,98,8,128]{3,2,1,0:T(8,128)S(1)}, f32[9,98,8,128]{3,2,1,0:T(8,128)}, u32[]{:S(2)}) copy-start(f32[9,98,8,128]{3,2,1,0:T(8,128)} %constant.17.clone.green_hbm) | copy-start | bytes 10838020
  2.7 1.4 %copy-start.1 = (f32[1024,384]{1,0:T(8,128)S(1)}, f32[1024,384]{1,0:T(8,128)}, u32[]{:S(2)}) copy-start(f32[1024,384]{1,0:T(8,128)} %constant.16.clone.iz_hbm) | copy-start | bytes 4718596
  4.1 1.4 %copy-start.2 = (f32[384,1024]{1,0:T(8,128)S(1)}, f32[384,1024]{1,0:T(8,128)}, u32[]{:S(2)}) copy-start(f32[384,1024]{1,0:T(8,128)} %constant.13.clone.fz_hbm) | copy-start | bytes 4718596
  5.5 1.2 %copy-start.3 = (f32[2,4,3,9216]{3,1,2,0:T(4,128)S(1)}, f32[2,4,3,9216]{3,1,2,0:T(4,128)}, u32[]{:S(2)}) copy-start(f32[2,4,3,9216]{3,1,2,0:T(4,128)} %param.9) | copy-start | bytes 2654212
  6.6 1.2 %copy-start.4 = (bf16[1152,384]{1,0:T(8,128)(2,1)S(1)}, bf16[1152,384]{1,0:T(8,128)(2,1)}, u32[]{:S(2)}) copy-start(bf16[1152,384]{1,0:T(8,128)(2,1)} %constant.12.clone.band_hbm) | copy-start | bytes 2654212
  7.8 0.9 %copy-start.5 = (f32[3,9216]{1,0:T(4,128)S(1)}, f32[3,9216]{1,0:T(4,128)}, u32[]{:S(2)}) copy-start(f32[3,9216]{1,0:T(4,128)} %pot_ref.1) | copy-start | bytes 331780
  8.7 0.8 copy-start.6
  9.5 0.8 copy-start.7
  10.3 0.7 copy-start.8

commit v2 on v1

--- a/solution.py
+++ b/solution.py
@@ -65,6 +65,12 @@
     rows.append(np.where(cells % 2 == 0, 1.0, -1.0) / math.sqrt(length))
     waves.append(length // 2)
     return np.stack(rows), (2.0 * math.pi / length * np.array(waves)) ** 2
+
+
+def split(table):
+    high = table.astype(ml_dtypes.bfloat16)
+    low = (table - high.astype(np.float64)).astype(ml_dtypes.bfloat16)
+    return high, low
 
 
 def transform_tables():
@@ -87,14 +93,16 @@
     total = along[:, None, None] + across
     kernel = np.where(total > 0, 4.0 * math.pi / np.where(total > 0, total, 1.0), 0.0)
     green = np.real(np.fft.ifft(kernel, axis=0))
-    green = green[(np.arange(NX + 2) - 2) % NX]
-    green = green.reshape(NX + 2, OWNERS, 8, 128).transpose(1, 0, 2, 3)
+    green = green[(np.arange(NX + 5) - 5) % NX]
+    green = green.reshape(NX + 5, OWNERS, 8, 128).transpose(1, 0, 2, 3)
     f32 = np.float32
+    y_high, y_low = split(forward_y.T)
+    z_high, z_low = split(forward_z.T)
     return (
         forward_z.astype(f32),
         forward_y.astype(f32),
-        forward_y.T.copy().astype(f32),
-        forward_z.T.copy().astype(f32),
+        np.concatenate([y_high, y_low], axis=1),
+        np.concatenate([z_high, z_low], axis=0),
         green.astype(f32),
     )
 
@@ -110,13 +118,14 @@
 
 
 def body(
-    orb_hbm, pot_ref, occ_ref, band_hbm, fz_hbm, fy_hbm, iy_hbm, iz_hbm, green_hbm,
+    orb_hbm, pot_hbm, occ_ref, band_hbm, fz_hbm, fy_hbm, iy_hbm, iz_hbm, green_hbm,
     prop_hbm, dens_ref, hart_ref,
-    field, first, prop, own0, own1, rim0, rim1, lines,
+    pot_ref, field, first, prop, own0, own1, rim0, rim1, lines,
     band_ref, fz_ref, fy_ref, iy_ref, iz_ref, green_ref,
-    modes, shares, summed, layer, answer, dens_modes, hart_modes,
-    load_sem, table_sem, store_sem, halo_send, halo_recv,
-    share_send, share_recv, layer_send, layer_recv, dens_send, dens_recv, hart_send, hart_recv,
+    modes, shares, summed, layer, partial, crossed, dens_own, hart_own, dens_modes, hart_modes,
+    load_sem, table_sem, store_sem, halo_send, halo_recv, hand,
+    share_send, share_recv, layer_send, layer_recv, cross_sem,
+    dens_send, dens_recv, hart_send, hart_recv,
 ):
     s = lax.axis_index("space")
     z = lax.axis_index("band")
@@ -124,15 +133,37 @@
     f32 = jnp.float32
     bf16 = jnp.bfloat16
 
-    loads = [
-        pltpu.make_async_copy(orb_hbm.at[part], field.at[:, pl.ds(4 * part, 4), :], load_sem.at[part])
-        for part in range(2)
-    ]
-    for copy in loads:
-        copy.start()
+    def lanes_of(c, extra=0, size=CHUNK):
+        return pl.ds(pl.multiple_of(c * CHUNK + extra, 128), size)
+
+    def load(c, half, part):
+        lanes = lanes_of(c, half * FOLD)
+        return pltpu.make_async_copy(
+            orb_hbm.at[part, :, :, lanes],
+            field.at[:, pl.ds(4 * part, 4), lanes],
+            load_sem.at[c, half, part],
+        )
+
+    barrier = pltpu.get_barrier_semaphore()
+
+    def greet(sem, axis, me, size, offset):
+        for step in (offset, size - offset):
+            pl.semaphore_signal(
+                sem, inc=1, device_id={axis: lax.rem(me + step, size)}, device_id_type=MESH
+            )
+
+    for offset in (1, 2):
+        greet(barrier, "space", s, SPACE, offset)
+        greet(barrier, "band", z, BAND, offset)
+    for c in range(CHUNKS):
+        for half in range(2):
+            for part in range(2):
+                load(c, half, part).start()
     owner = (OWNERS * z + BAND - 1) // BAND
     owner_index = jnp.minimum(owner, OWNERS - 1)
     is_owner = (BAND * owner) // OWNERS == z
+    pot_copy = pltpu.make_async_copy(pot_hbm, pot_ref, table_sem.at[6])
+    pot_copy.start()
     tables = [
         pltpu.make_async_copy(src, dst, table_sem.at[i])
         for i, (src, dst) in enumerate(
@@ -146,28 +177,7 @@
             ]
         )
     ]
-    for copy in tables:
-        copy.start()
-
-    barrier = pltpu.get_barrier_semaphore()
-
-    def greet_space(k, carry):
-        pl.semaphore_signal(
-            barrier, inc=1, device_id={"space": lax.rem(s + k, SPACE)}, device_id_type=MESH
-        )
-        return carry
-
-    def greet_band(k, carry):
-        pl.semaphore_signal(
-            barrier, inc=1, device_id={"band": lax.rem(z + k, BAND)}, device_id_type=MESH
-        )
-        return carry
-
-    lax.fori_loop(1, BAND, greet_band, 0)
-    lax.fori_loop(1, SPACE, greet_space, 0)
-
-    def lanes_of(c, extra=0, size=CHUNK):
-        return pl.ds(pl.multiple_of(c * CHUNK + extra, 128), size)
+    tables[0].start()
 
     outward = 2 * core - 1
     owns = (own0, own1)
@@ -212,23 +222,33 @@
                 [source[p, :, FOLD : FOLD + BLOCK], zeros], axis=0
             ).astype(bf16)
 
-    for copy in loads:
-        copy.wait()
-    pl.semaphore_wait(barrier, SPACE + BAND - 2)
-
-    def ship(c, carry):
+    def pack(c, carry):
+        for half in range(2):
+            for part in range(2):
+                load(c, half, part).wait()
         for p in range(PLANES):
             own0[p, :, lanes_of(c, BLOCK)] = jnp.concatenate(
                 [field[p, :, lanes_of(c)], field[p, :, lanes_of(c, FOLD)]], axis=0
             ).astype(bf16)
+        return carry
+
+    lax.fori_loop(0, CHUNKS, pack, 0)
+    pl.semaphore_wait(barrier, 8)
+
+    def ship(c, carry):
         for kind in range(3):
             halo(0, kind, c).start()
         return carry
 
     lax.fori_loop(0, CHUNKS, ship, 0)
+    greet(hand.at[0], "band", z, BAND, 2)
+    greet(hand.at[1], "space", s, SPACE, 2)
     fold_edges(field, own0)
+    for copy in tables[1:]:
+        copy.start()
     tables[0].wait()
 
+    pot_copy.wait()
     near_left = jnp.where(s >= 1, 1.0, 0.0).astype(f32)
     far_left = jnp.where(s >= 2, 1.0, 0.0).astype(f32)
     near_right = jnp.where(s <= SPACE - 2, 1.0, 0.0).astype(f32)
@@ -276,6 +296,7 @@
                     value = centre * factor - across[8 * half : 8 * half + 8]
                     finish(p, b, half, lanes, centre, value)
 
+
     def first_chunk(c, carry):
         arrive(0, c)
         values = {}
@@ -294,6 +315,10 @@
         return carry
 
     lax.fori_loop(0, CHUNKS, first_chunk, 0)
+    pl.semaphore_wait(hand.at[0], 2)
+    greet(hand.at[2], "band", z, BAND, 4)
+    pl.semaphore_wait(hand.at[1], 2)
+    greet(hand.at[3], "space", s, SPACE, 4)
     fold_edges(first, own1)
 
     rows = lax.broadcasted_iota(jnp.int32, (FIELDS, BLOCK), 0)
@@ -331,6 +356,9 @@
         return carry
 
     lax.fori_loop(0, CHUNKS, second_chunk, 0)
+    pl.semaphore_wait(hand.at[2], 2)
+    pl.semaphore_wait(hand.at[3], 2)
+    greet(hand.at[4], "space", s, SPACE, 8)
 
     for copy in tables[1:]:
         copy.wait()
@@ -362,6 +390,7 @@
         for o in range(3):
             modes[6 + o, p] = rest[8 * o : 8 * o + 8]
 
+
     def share_copy(o, source):
         return pltpu.make_async_remote_copy(
             src_ref=modes.at[o],
@@ -372,20 +401,40 @@
             device_id_type=MESH,
         )
 
-    for o in range(OWNERS):
-        @pl.when((BAND * o) // OWNERS != z)
+    def by_distance(i, middle):
+        return middle + jnp.where(lax.rem(i, 2) == 0, i // 2, -(i + 1) // 2)
+
+    def out_share(i, carry):
+        target = lax.rem(z + by_distance(i, BAND // 2), BAND)
+        o = (OWNERS * target + BAND - 1) // BAND
+
+        @pl.when((BAND * o) // OWNERS == target)
         def _():
             share_copy(o, z).start()
+
+        return carry
+
+    lax.fori_loop(0, BAND - 1, out_share, 0)
+    pl.semaphore_wait(hand.at[4], 2)
 
     def layer_copy(k):
         return pltpu.make_async_remote_copy(
             src_ref=summed,
-            dst_ref=layer.at[SPACE - k],
+            dst_ref=layer.at[SPACE // 2 - k],
             send_sem=layer_send.at[k],
-            recv_sem=layer_recv.at[SPACE - k],
-            device_id={"space": lax.rem(s + k, SPACE)},
+            recv_sem=layer_recv.at[SPACE // 2 - k],
+            device_id={"space": lax.rem(s + 2 * k, SPACE)},
             device_id_type=MESH,
         )
+
+    partner_copy = pltpu.make_async_remote_copy(
+        src_ref=partial,
+        dst_ref=crossed,
+        send_sem=cross_sem.at[0],
+        recv_sem=cross_sem.at[1],
+        device_id={"space": s - outward},
+        device_id_type=MESH,
+    )
 
     def band_copy(src, dst, send, recv, k):
         return pltpu.make_async_remote_copy(
@@ -397,6 +446,13 @@
             device_id_type=MESH,
         )
 
+    def keep(values, ref, gathered_ref):
+        upper = jnp.concatenate([values[0], values[1]], axis=0).astype(bf16)
+        lower = jnp.concatenate([values[2], jnp.zeros((8, 128), f32)], axis=0).astype(bf16)
+        for out in (ref, gathered_ref.at[owner_index]):
+            out[0] = upper
+            out[1] = lower
+
     @pl.when(is_owner)
     def _():
         def collect(k, total):
@@ -407,26 +463,28 @@
         total = lax.fori_loop(1, BAND, collect, modes[owner_index])
         summed[...] = total
         layer[0] = total
-        dens_modes[owner_index] = total
-
-        def out_layer(k, carry):
-            layer_copy(k).start()
+
+        def out_layer(i, carry):
+            layer_copy(by_distance(i, SPACE // 4)).start()
             return carry
 
-        lax.fori_loop(1, SPACE, out_layer, 0)
-
-        def out_dens(k, carry):
-            band_copy(summed, dens_modes, dens_send, dens_recv, k).start()
+        lax.fori_loop(0, SPACE // 2 - 1, out_layer, 0)
+        keep([total[p] for p in range(PLANES)], dens_own, dens_modes)
+
+        def out_dens(i, carry):
+            band_copy(dens_own, dens_modes, dens_send, dens_recv, by_distance(i, BAND // 2)).start()
             return carry
 
-        lax.fori_loop(1, BAND, out_dens, 0)
+        lax.fori_loop(0, BAND - 1, out_dens, 0)
 
         def apply(r, total):
             out = list(total)
             for q in range(PLANES):
                 value = layer[r, q]
                 for p in range(PLANES):
-                    out[p] = out[p] + green_ref[3 * r + q - p + 2] * value
+                    at = 6 * r + q - p + 5
+                    out[p] = out[p] + green_ref[at] * value
+                    out[PLANES + p] = out[PLANES + p] + green_ref[at + 3 * outward] * value
             return tuple(out)
 
         def collect_layer(r, total):
@@ -434,30 +492,34 @@
             return apply(r, total)
 
         zero = jnp.zeros((8, 128), f32)
-        result = lax.fori_loop(1, SPACE, collect_layer, apply(0, (zero, zero, zero)))
+        result = lax.fori_loop(1, SPACE // 2, collect_layer, apply(0, (zero,) * (2 * PLANES)))
         for p in range(PLANES):
-            answer[p] = result[p]
-            hart_modes[owner_index, p] = result[p]
-
-        def out_hart(k, carry):
-            band_copy(answer, hart_modes, hart_send, hart_recv, k).start()
+            partial[p] = result[PLANES + p]
+        partner_copy.start()
+        partner_copy.wait()
+        keep([result[p] + crossed[p] for p in range(PLANES)], hart_own, hart_modes)
+
+        def out_hart(i, carry):
+            band_copy(hart_own, hart_modes, hart_send, hart_recv, by_distance(i, BAND // 2)).start()
             return carry
 
-        lax.fori_loop(1, BAND, out_hart, 0)
+        lax.fori_loop(0, BAND - 1, out_hart, 0)
 
     def back(spec_ref):
+        halves = [[spec_ref[o, i].astype(f32) for i in range(2)] for o in range(OWNERS)]
         pieces = []
         for p in range(PLANES):
-            head = jnp.concatenate([spec_ref[o, p] for o in range(6)], axis=0)
-            rest = jnp.concatenate([spec_ref[6 + o, p] for o in range(3)], axis=0)
-            upper = jnp.concatenate(
-                [jnp.where(lane < 64, head, 0.0), jnp.where(lane >= 64, head, 0.0)], axis=0
-            )
-            lower = jnp.concatenate(
-                [jnp.where(lane // 32 == quarter, rest, 0.0) for quarter in range(4)], axis=0
-            )
-            pieces += [upper, lower]
-        rows_y = exact_dot(iy_ref[...], jnp.concatenate(pieces, axis=1))
+            at = 8 * (p % 2)
+            blocks = [halves[o][p // 2][at : at + 8] for o in range(OWNERS)]
+            head = jnp.concatenate(blocks[:6], axis=0)
+            rest = jnp.concatenate(blocks[6:], axis=0)
+            upper = [jnp.where(lane < 64, head, 0.0), jnp.where(lane >= 64, head, 0.0)]
+            lower = [jnp.where(lane // 32 == quarter, rest, 0.0) for quarter in range(4)]
+            pieces += [jnp.concatenate(upper, axis=0), jnp.concatenate(lower, axis=0)]
+        spread = jnp.concatenate(pieces, axis=1).astype(bf16)
+        rows_y = jnp.dot(
+            iy_ref[...], jnp.concatenate([spread, spread], axis=0), preferred_element_type=f32
+        )
         flat = jnp.concatenate(
             [
                 jnp.concatenate(
@@ -471,7 +533,14 @@
             ],
             axis=0,
         )
-        return exact_dot(flat, iz_ref[...])
+        high = flat.astype(bf16)
+        low = (flat - high.astype(f32)).astype(bf16)
+        z_high = iz_ref[0:1024]
+        return (
+            jnp.dot(high, z_high, preferred_element_type=f32)
+            + jnp.dot(low, z_high, preferred_element_type=f32)
+            + jnp.dot(high, iz_ref[1024:2048], preferred_element_type=f32)
+        )
 
     def put(out_ref, values):
         for p in range(PLANES):
@@ -483,7 +552,7 @@
         for o in range(OWNERS):
             @pl.when((BAND * o) // OWNERS != z)
             def _():
-                pltpu.make_async_copy(summed, dst.at[o], recv.at[o]).wait()
+                pltpu.make_async_copy(dens_own, dst.at[o], recv.at[o]).wait()
 
     gathered(dens_modes, dens_recv)
     put(dens_ref, back(dens_modes))
@@ -496,11 +565,11 @@
             layer_copy(k).wait_send()
             return carry
 
-        lax.fori_loop(1, SPACE, drain_layer, 0)
+        lax.fori_loop(1, SPACE // 2, drain_layer, 0)
 
         def drain_band(k, carry):
-            band_copy(summed, dens_modes, dens_send, dens_recv, k).wait_send()
-            band_copy(answer, hart_modes, hart_send, hart_recv, k).wait_send()
+            band_copy(dens_own, dens_modes, dens_send, dens_recv, k).wait_send()
+            band_copy(hart_own, hart_modes, hart_send, hart_recv, k).wait_send()
             return carry
 
         lax.fori_loop(1, BAND, drain_band, 0)
@@ -522,6 +591,22 @@
     lax.fori_loop(0, CHUNKS, drain, 0)
 
 
+def settle(prop_in, dens_in, hart_in, prop_out, dens_out, hart_out, prop_at, dens_at, hart_at, in_sem, out_sem):
+    routes = [(dens_in, dens_at, dens_out), (hart_in, hart_at, hart_out)]
+    for part in range(2):
+        for p in range(PLANES):
+            routes.append((prop_in.at[part, p], prop_at.at[part, p], prop_out.at[part, p]))
+    inward = [pltpu.make_async_copy(r[0], r[1], in_sem.at[i]) for i, r in enumerate(routes)]
+    outward = [pltpu.make_async_copy(r[1], r[2], out_sem.at[i]) for i, r in enumerate(routes)]
+    for copy in inward:
+        copy.start()
+    for i in range(len(routes)):
+        inward[i].wait()
+        outward[i].start()
+    for copy in outward:
+        copy.wait()
+
+
 def per_device(orbitals, potential, occupations):
     f32 = jnp.float32
     bf16 = jnp.bfloat16
@@ -530,16 +615,18 @@
     dma = pltpu.SemaphoreType.DMA
     anywhere = pl.BlockSpec(memory_space=pl.ANY)
     whole = pl.BlockSpec(memory_space=pltpu.VMEM)
-    prop, dens, hart = pl.pallas_call(
+    in_hbm = pl.BlockSpec(memory_space=pltpu.HBM)
+    raw = pl.pallas_call(
         body,
         out_shape=(
             jax.ShapeDtypeStruct((2, PLANES, 4, CELLS), f32),
             jax.ShapeDtypeStruct((PLANES, CELLS), f32),
             jax.ShapeDtypeStruct((PLANES, CELLS), f32),
         ),
-        in_specs=[anywhere, whole, pl.BlockSpec(memory_space=pltpu.SMEM)] + [anywhere] * 6,
+        in_specs=[in_hbm, in_hbm, pl.BlockSpec(memory_space=pltpu.SMEM)] + [in_hbm] * 6,
         out_specs=(anywhere, whole, whole),
         scratch_shapes=[
+            vmem((PLANES, CELLS), f32),
             vmem((PLANES, FIELDS, CELLS), f32),
             vmem((PLANES, FIELDS, CELLS), f32),
             vmem((PLANES, FIELDS, CELLS), f32),
@@ -551,32 +638,37 @@
             vmem((WINDOW, BLOCK), bf16),
             vmem((BLOCK, 1024), f32),
             vmem((NY, NY), f32),
-            vmem((NY, NY), f32),
-            vmem((1024, BLOCK), f32),
-            vmem((NX + 2, 8, 128), f32),
+            vmem((NY, 2 * NY), bf16),
+            vmem((2048, BLOCK), bf16),
+            vmem((NX + 5, 8, 128), f32),
             vmem((OWNERS, PLANES, 8, 128), f32),
             vmem((BAND, PLANES, 8, 128), f32),
             vmem((PLANES, 8, 128), f32),
-            vmem((SPACE, PLANES, 8, 128), f32),
+            vmem((SPACE // 2, PLANES, 8, 128), f32),
             vmem((PLANES, 8, 128), f32),
-            vmem((OWNERS, PLANES, 8, 128), f32),
-            vmem((OWNERS, PLANES, 8, 128), f32),
-            dma((2,)),
-            dma((6,)),
+            vmem((PLANES, 8, 128), f32),
+            vmem((2, 16, 128), bf16),
+            vmem((2, 16, 128), bf16),
+            vmem((OWNERS, 2, 16, 128), bf16),
+            vmem((OWNERS, 2, 16, 128), bf16),
+            dma((CHUNKS, 2, 2)),
+            dma((7,)),
             dma((CHUNKS, 2, 2)),
             dma((2, 4, CHUNKS)),
             dma((2, 4, CHUNKS)),
+            pltpu.SemaphoreType.REGULAR((5,)),
             dma((OWNERS,)),
             dma((BAND,)),
-            dma((SPACE,)),
-            dma((SPACE,)),
+            dma((SPACE // 2,)),
+            dma((SPACE // 2,)),
+            dma((2,)),
             dma((BAND,)),
             dma((OWNERS,)),
             dma((BAND,)),
             dma((OWNERS,)),
         ],
         compiler_params=pltpu.CompilerParams(
-            collective_id=0, has_side_effects=True, vmem_limit_bytes=40 * 2**20
+            collective_id=0, has_side_effects=True, vmem_limit_bytes=62 * 2**20
         ),
     )(
         jnp.transpose(orbitals, (0, 2, 1, 3)),
@@ -589,6 +681,14 @@
         jnp.asarray(inverse_z),
         jnp.asarray(green),
     )
+    prop, dens, hart = pl.pallas_call(
+        settle,
+        out_shape=[jax.ShapeDtypeStruct(r.shape, r.dtype) for r in raw],
+        in_specs=[anywhere] * 3,
+        out_specs=[anywhere] * 3,
+        scratch_shapes=[vmem(r.shape, r.dtype) for r in raw] + [dma((8,)), dma((8,))],
+        compiler_params=pltpu.CompilerParams(vmem_limit_bytes=62 * 2**20),
+    )(*raw)
     return jnp.transpose(prop, (0, 2, 1, 3)), dens, hart
 
 

time: 82.4 us -> 63.3 us (0.77)
  local copies, waits for them, and re-layouts: 12.6 us -> 0 us
  Pallas kernels: 68.7 us -> 62.5 us
    unnamed x21 -> x0, local copies, waits for them, and re-layouts: 12.6 us -> none
    pallas_call x1, Pallas kernels: 68.7 us -> 60.3 us  [per_device(): pl.pallas_call(body, out_shape=(jax.ShapeDtypeStruct((2, PLANES, 4, CELLS...]
    pallas_call x0 -> x1, Pallas kernels: none -> 2.15 us  [per_device(): pl.pallas_call(settle, out_shape=[jax.ShapeDtypeStruct(r.shape, r.dtype)...]
where the time goes in v2:
time: 63.3 us; the launch traced here: 63.1 us
  Pallas kernels  62.5 us (99%)
  between operations  0.64 us (1%)
    pallas_call x1, Pallas kernels, per_device(): pl.pallas_call(body, out_shape=(jax.ShapeDtypeStruct((2, PLANES, 4, CELLS...  60.3 us
    pallas_call x1, Pallas kernels, per_device(): pl.pallas_call(settle, out_shape=[jax.ShapeDtypeStruct(r.shape, r.dtype)...  2.15 us

profile of v2, /device:TPU:1, one launch (start us, length us, event | category | flops | bytes accessed | tf_op | source)
XLA Modules:
  0.0 63.1 jit_solution(14026435642915878928)
XLA Ops:
  0.6 60.3 %shard_map.112 = (f32[2,3,4,9216]{3,2,1,0:T(4,128)}, f32[3,9216]{1,0:T(4,128)}, f32[3,9216]{1,0:T(4,128)}) custom-call(f32[2,3,4,9216]{3,2,1,0:T(4,128)} %bitcast.2, f32[3,9216]{1,0:T(4,128)} %pot_hbm.1, f32[4]{0:T(128)} %occ_ref.1, bf16[1152,384]{1,0:T(8,128)(2,1)} %constant.12.clone.band_hbm, f32[384,1024]{1,0:T(8,128)} %constant.13.clone.fz_hbm, ...), custom_call_target="tpu_custom_call" | custom-call | tf_op jit(solution)/shard_map/pallas_call | solution.py:619
  60.9 2.1 %shard_map.113 = (f32[2,3,4,9216]{3,2,1,0:T(4,128)}, f32[3,9216]{1,0:T(4,128)}, f32[3,9216]{1,0:T(4,128)}) custom-call(f32[2,3,4,9216]{3,2,1,0:T(4,128)} %get-tuple-element.9.prop_in, f32[3,9216]{1,0:T(4,128)} %get-tuple-element.10.dens_in, f32[3,9216]{1,0:T(4,128)} %get-tuple-element.11.hart_in), custom_call_target="tpu_custom_call" | custom-call | tf_op jit(solution)/shard_map/pallas_call | solution.py:684

commit v3 on v2

--- a/solution.py
+++ b/solution.py
@@ -118,9 +118,9 @@
 
 
 def body(
-    orb_hbm, pot_hbm, occ_ref, band_hbm, fz_hbm, fy_hbm, iy_hbm, iz_hbm, green_hbm,
-    prop_hbm, dens_ref, hart_ref,
-    pot_ref, field, first, prop, own0, own1, rim0, rim1, lines,
+    orb_hbm, pot_hbm, occ_hbm, band_hbm, fz_hbm, fy_hbm, iy_hbm, iz_hbm, green_hbm,
+    prop_hbm, dens_hbm, hart_hbm,
+    pot_ref, occ_ref, dens_ref, hart_ref, field, first, prop, own0, own1, rim0, rim1, lines,
     band_ref, fz_ref, fy_ref, iy_ref, iz_ref, green_ref,
     modes, shares, summed, layer, partial, crossed, dens_own, hart_own, dens_modes, hart_modes,
     load_sem, table_sem, store_sem, halo_send, halo_recv, hand,
@@ -164,6 +164,8 @@
     is_owner = (BAND * owner) // OWNERS == z
     pot_copy = pltpu.make_async_copy(pot_hbm, pot_ref, table_sem.at[6])
     pot_copy.start()
+    occ_copy = pltpu.make_async_copy(occ_hbm, occ_ref, table_sem.at[7])
+    occ_copy.start()
     tables = [
         pltpu.make_async_copy(src, dst, table_sem.at[i])
         for i, (src, dst) in enumerate(
@@ -249,64 +251,74 @@
     tables[0].wait()
 
     pot_copy.wait()
-    near_left = jnp.where(s >= 1, 1.0, 0.0).astype(f32)
-    far_left = jnp.where(s >= 2, 1.0, 0.0).astype(f32)
-    near_right = jnp.where(s <= SPACE - 2, 1.0, 0.0).astype(f32)
-    far_right = jnp.where(s <= SPACE - 3, 1.0, 0.0).astype(f32)
-    left_weights = (far_left, near_left, near_left, near_left)
-    right_weights = (near_right, near_right, near_right, far_right)
+    occ_copy.wait()
+    edge = (s - core) // 2
+    before = jnp.where(edge >= 1, 1.0, 0.0).astype(f32)
+    after = jnp.where(edge <= SPACE // 2 - 2, 1.0, 0.0).astype(f32)
+    outer_weight = jnp.where(core == 0, before, after)
+    inner_weight = jnp.where(core == 0, after, before)
 
     gain = stencil_coeffs[1] / (2.0 * energy_scale)
     level = -(energy_shift + 1.5 * stencil_coeffs[0]) / energy_scale
 
-    def arrive(phase, c):
-        halo(phase, 0, c).wait_recv()
-        halo(phase, 3, c).start()
-        for kind in (1, 2, 3):
-            halo(phase, kind, c).wait_recv()
+    def mirrored(position, last):
+        return position + core * (last - 2 * position)
 
     def stencil(phase, source, c, finish):
         own, rim = owns[phase], rims[phase]
         windows = [
-            own[p, :, lanes_of(c, b * BLOCK, WINDOW)]
-            for p in range(PLANES)
+            own[mirrored(q, 2), :, lanes_of(c, b * BLOCK, WINDOW)]
+            for q in range(PLANES)
             for b in range(PER_CHUNK)
         ]
         flat = jnp.dot(
             jnp.concatenate(windows, axis=0), band_ref[...], preferred_element_type=f32
         )
-        for b in range(PER_CHUNK):
-            outside = lanes_of(c, b * BLOCK, BLOCK)
-            inside = lanes_of(c, (b + 1) * BLOCK, BLOCK)
-            stack = [rim[0, k, :, outside].astype(f32) * left_weights[k] for k in range(4)]
-            stack += [own[p, :, inside].astype(f32) for p in range(PLANES)]
-            stack += [rim[1, k, :, outside].astype(f32) * right_weights[k] for k in range(4)]
-            for p in range(PLANES):
-                across = stack[p + 5] + stack[p + 3]
-                for offset in range(2, 5):
-                    across = across + scaled_coeffs[offset] * (
-                        stack[p + 4 + offset] + stack[p + 4 - offset]
-                    )
-                at = 16 * (p * PER_CHUNK + b)
-                across = gain * (across + flat[at : at + 16])
-                for half in range(2):
-                    lanes = lanes_of(c, half * FOLD + b * BLOCK, BLOCK)
-                    centre = source[p, :, lanes]
-                    factor = pot_ref[p : p + 1, lanes] * (1.0 / energy_scale) + level
-                    value = centre * factor - across[8 * half : 8 * half + 8]
-                    finish(p, b, half, lanes, centre, value)
+        halo(phase, 0, c).wait_recv()
+        halo(phase, 3, c).start()
+        for kind in (1, 2):
+            halo(phase, kind, c).wait_recv()
+        for targets in ((0, 1), (2,)):
+            if 2 in targets:
+                halo(phase, 3, c).wait_recv()
+            for b in range(PER_CHUNK):
+                outside = lanes_of(c, b * BLOCK, BLOCK)
+                inside = lanes_of(c, (b + 1) * BLOCK, BLOCK)
+                stack = {}
+                for at in range(targets[0], targets[-1] + 9):
+                    if at < 4:
+                        plane = rim[core, mirrored(at, 3), :, outside].astype(f32) * outer_weight
+                    elif at < 7:
+                        plane = own[mirrored(at - 4, 2), :, inside].astype(f32)
+                    else:
+                        plane = rim[1 - core, mirrored(at - 7, 3), :, outside].astype(f32)
+                    stack[at] = plane * inner_weight if at == 10 else plane
+                for q in targets:
+                    p = mirrored(q, 2)
+                    across = stack[q + 5] + stack[q + 3]
+                    for offset in range(2, 5):
+                        across = across + scaled_coeffs[offset] * (
+                            stack[q + 4 + offset] + stack[q + 4 - offset]
+                        )
+                    at = 16 * (q * PER_CHUNK + b)
+                    across = gain * (across + flat[at : at + 16])
+                    for half in range(2):
+                        lanes = lanes_of(c, half * FOLD + b * BLOCK, BLOCK)
+                        centre = source[p, :, lanes]
+                        factor = pot_ref[pl.ds(p, 1), lanes] * (1.0 / energy_scale) + level
+                        value = centre * factor - across[8 * half : 8 * half + 8]
+                        finish(p, b, half, lanes, centre, value)
 
 
     def first_chunk(c, carry):
-        arrive(0, c)
-        values = {}
+        values = []
 
         def finish(p, b, half, lanes, centre, value):
             first[p, :, lanes] = value
-            values[p, b, half] = value
+            values.append(value)
             if half == 1:
                 own1[p, :, lanes_of(c, (b + 1) * BLOCK, BLOCK)] = jnp.concatenate(
-                    [values[p, b, 0], value], axis=0
+                    values[-2:], axis=0
                 ).astype(bf16)
 
         stencil(0, field, c, finish)
@@ -336,8 +348,6 @@
         )
 
     def second_chunk(c, carry):
-        arrive(1, c)
-
         def finish(p, b, half, lanes, centre, value):
             swapped = jnp.concatenate([centre[4:8], centre[0:4]], axis=0)
             result = (
@@ -554,10 +564,14 @@
             def _():
                 pltpu.make_async_copy(dens_own, dst.at[o], recv.at[o]).wait()
 
+    dens_copy = pltpu.make_async_copy(dens_ref, dens_hbm, table_sem.at[8])
+    hart_copy = pltpu.make_async_copy(hart_ref, hart_hbm, table_sem.at[9])
     gathered(dens_modes, dens_recv)
     put(dens_ref, back(dens_modes))
+    dens_copy.start()
     gathered(hart_modes, hart_recv)
     put(hart_ref, back(hart_modes))
+    hart_copy.start()
 
     @pl.when(is_owner)
     def _():
@@ -589,6 +603,8 @@
         return carry
 
     lax.fori_loop(0, CHUNKS, drain, 0)
+    dens_copy.wait()
+    hart_copy.wait()
 
 
 def settle(prop_in, dens_in, hart_in, prop_out, dens_out, hart_out, prop_at, dens_at, hart_at, in_sem, out_sem):
@@ -614,8 +630,6 @@
     vmem = pltpu.VMEM
     dma = pltpu.SemaphoreType.DMA
     anywhere = pl.BlockSpec(memory_space=pl.ANY)
-    whole = pl.BlockSpec(memory_space=pltpu.VMEM)
-    in_hbm = pl.BlockSpec(memory_space=pltpu.HBM)
     raw = pl.pallas_call(
         body,
         out_shape=(
@@ -623,9 +637,12 @@
             jax.ShapeDtypeStruct((PLANES, CELLS), f32),
             jax.ShapeDtypeStruct((PLANES, CELLS), f32),
         ),
-        in_specs=[in_hbm, in_hbm, pl.BlockSpec(memory_space=pltpu.SMEM)] + [in_hbm] * 6,
-        out_specs=(anywhere, whole, whole),
+        in_specs=[anywhere] * 9,
+        out_specs=(anywhere, anywhere, anywhere),
         scratch_shapes=[
+            vmem((PLANES, CELLS), f32),
+            pltpu.SMEM((4,), f32),
+            vmem((PLANES, CELLS), f32),
             vmem((PLANES, CELLS), f32),
             vmem((PLANES, FIELDS, CELLS), f32),
             vmem((PLANES, FIELDS, CELLS), f32),
@@ -652,7 +669,7 @@
             vmem((OWNERS, 2, 16, 128), bf16),
             vmem((OWNERS, 2, 16, 128), bf16),
             dma((CHUNKS, 2, 2)),
-            dma((7,)),
+            dma((10,)),
             dma((CHUNKS, 2, 2)),
             dma((2, 4, CHUNKS)),
             dma((2, 4, CHUNKS)),

time: 63.3 us -> 61.8 us (0.976)
  Pallas kernels: 62.5 us -> 60.6 us
    pallas_call x1, Pallas kernels: 60.3 us -> 58.4 us  [per_device(): pl.pallas_call(body, out_shape=(jax.ShapeDtypeStruct((2, PLANES, 4, CELLS...]
where the time goes in v3:
time: 61.8 us; the launch traced here: 61.2 us
  Pallas kernels  60.6 us (98%)
  between operations  0.64 us (1%)
    pallas_call x1, Pallas kernels, per_device(): pl.pallas_call(body, out_shape=(jax.ShapeDtypeStruct((2, PLANES, 4, CELLS...  58.4 us
    pallas_call x1, Pallas kernels, per_device(): pl.pallas_call(settle, out_shape=[jax.ShapeDtypeStruct(r.shape, r.dtype)...  2.15 us

profile of v3, /device:TPU:1, one launch (start us, length us, event | category | flops | bytes accessed | tf_op | source)
XLA Modules:
  0.0 61.2 jit_solution(5672698421978078169)
XLA Ops:
  0.6 58.4 %shard_map.112 = (f32[2,3,4,9216]{3,2,1,0:T(4,128)}, f32[3,9216]{1,0:T(4,128)}, f32[3,9216]{1,0:T(4,128)}) custom-call(f32[2,3,4,9216]{3,2,1,0:T(4,128)} %bitcast.2, f32[3,9216]{1,0:T(4,128)} %pot_hbm.1, f32[4]{0:T(128)} %occ_hbm.1, bf16[1152,384]{1,0:T(8,128)(2,1)} %constant.12.clone.band_hbm, f32[384,1024]{1,0:T(8,128)} %constant.13.clone.fz_hbm, ...), custom_call_target="tpu_custom_call" | custom-call | tf_op jit(solution)/shard_map/pallas_call | solution.py:633
  59.1 2.1 %shard_map.113 = (f32[2,3,4,9216]{3,2,1,0:T(4,128)}, f32[3,9216]{1,0:T(4,128)}, f32[3,9216]{1,0:T(4,128)}) custom-call(f32[2,3,4,9216]{3,2,1,0:T(4,128)} %get-tuple-element.9.prop_in, f32[3,9216]{1,0:T(4,128)} %get-tuple-element.10.dens_in, f32[3,9216]{1,0:T(4,128)} %get-tuple-element.11.hart_in), custom_call_target="tpu_custom_call" | custom-call | tf_op jit(solution)/shard_map/pallas_call | solution.py:701

commit v4 on v3

--- a/solution.py
+++ b/solution.py
@@ -99,10 +99,8 @@
     y_high, y_low = split(forward_y.T)
     z_high, z_low = split(forward_z.T)
     return (
-        forward_z.astype(f32),
-        forward_y.astype(f32),
-        np.concatenate([y_high, y_low], axis=1),
-        np.concatenate([z_high, z_low], axis=0),
+        np.concatenate([forward_z, np.pad(forward_y, ((0, 0), (0, 1024 - NY)))]).astype(f32),
+        np.concatenate([z_high, z_low, np.pad(np.concatenate([y_high, y_low], axis=1), ((0, 0), (0, BLOCK - 2 * NY)))]),
         green.astype(f32),
     )
 
@@ -118,10 +116,10 @@
 
 
 def body(
-    orb_hbm, pot_hbm, occ_hbm, band_hbm, fz_hbm, fy_hbm, iy_hbm, iz_hbm, green_hbm,
+    orb_hbm, pot_hbm, occ_hbm, band_hbm, forward_hbm, inverse_hbm, green_hbm,
     prop_hbm, dens_hbm, hart_hbm,
-    pot_ref, occ_ref, dens_ref, hart_ref, field, first, prop, own0, own1, rim0, rim1, lines,
-    band_ref, fz_ref, fy_ref, iy_ref, iz_ref, green_ref,
+    pot_ref, occ_ref, dens_ref, hart_ref, flat, field, first, prop, own0, own1, rim0, rim1, lines,
+    band_ref, forward_ref, inverse_ref, green_ref,
     modes, shares, summed, layer, partial, crossed, dens_own, hart_own, dens_modes, hart_modes,
     load_sem, table_sem, store_sem, halo_send, halo_recv, hand,
     share_send, share_recv, layer_send, layer_recv, cross_sem,
@@ -162,19 +160,17 @@
     owner = (OWNERS * z + BAND - 1) // BAND
     owner_index = jnp.minimum(owner, OWNERS - 1)
     is_owner = (BAND * owner) // OWNERS == z
-    pot_copy = pltpu.make_async_copy(pot_hbm, pot_ref, table_sem.at[6])
+    pot_copy = pltpu.make_async_copy(pot_hbm, pot_ref, table_sem.at[4])
     pot_copy.start()
-    occ_copy = pltpu.make_async_copy(occ_hbm, occ_ref, table_sem.at[7])
+    occ_copy = pltpu.make_async_copy(occ_hbm, occ_ref, table_sem.at[5])
     occ_copy.start()
     tables = [
         pltpu.make_async_copy(src, dst, table_sem.at[i])
         for i, (src, dst) in enumerate(
             [
                 (band_hbm, band_ref),
-                (fz_hbm, fz_ref),
-                (fy_hbm, fy_ref),
-                (iy_hbm, iy_ref),
-                (iz_hbm, iz_ref),
+                (forward_hbm, forward_ref),
+                (inverse_hbm, inverse_ref),
                 (green_hbm.at[owner_index], green_ref),
             ]
         )
@@ -264,53 +260,65 @@
     def mirrored(position, last):
         return position + core * (last - 2 * position)
 
-    def stencil(phase, source, c, finish):
-        own, rim = owns[phase], rims[phase]
+    def receive(phase, c):
+        own = owns[phase]
         windows = [
             own[mirrored(q, 2), :, lanes_of(c, b * BLOCK, WINDOW)]
             for q in range(PLANES)
             for b in range(PER_CHUNK)
         ]
-        flat = jnp.dot(
+        flat[lax.rem(c, 2)] = jnp.dot(
             jnp.concatenate(windows, axis=0), band_ref[...], preferred_element_type=f32
         )
         halo(phase, 0, c).wait_recv()
         halo(phase, 3, c).start()
-        for kind in (1, 2):
+
+    def stencil(phase, source, c, finish):
+        own, rim = owns[phase], rims[phase]
+        slot = lax.rem(c, 2)
+        for kind in (1, 2, 3):
             halo(phase, kind, c).wait_recv()
-        for targets in ((0, 1), (2,)):
-            if 2 in targets:
-                halo(phase, 3, c).wait_recv()
-            for b in range(PER_CHUNK):
-                outside = lanes_of(c, b * BLOCK, BLOCK)
-                inside = lanes_of(c, (b + 1) * BLOCK, BLOCK)
-                stack = {}
-                for at in range(targets[0], targets[-1] + 9):
-                    if at < 4:
-                        plane = rim[core, mirrored(at, 3), :, outside].astype(f32) * outer_weight
-                    elif at < 7:
-                        plane = own[mirrored(at - 4, 2), :, inside].astype(f32)
-                    else:
-                        plane = rim[1 - core, mirrored(at - 7, 3), :, outside].astype(f32)
-                    stack[at] = plane * inner_weight if at == 10 else plane
-                for q in targets:
-                    p = mirrored(q, 2)
-                    across = stack[q + 5] + stack[q + 3]
-                    for offset in range(2, 5):
-                        across = across + scaled_coeffs[offset] * (
-                            stack[q + 4 + offset] + stack[q + 4 - offset]
-                        )
-                    at = 16 * (q * PER_CHUNK + b)
-                    across = gain * (across + flat[at : at + 16])
-                    for half in range(2):
-                        lanes = lanes_of(c, half * FOLD + b * BLOCK, BLOCK)
-                        centre = source[p, :, lanes]
-                        factor = pot_ref[pl.ds(p, 1), lanes] * (1.0 / energy_scale) + level
-                        value = centre * factor - across[8 * half : 8 * half + 8]
-                        finish(p, b, half, lanes, centre, value)
-
-
-    def first_chunk(c, carry):
+        for b in range(PER_CHUNK):
+            outside = lanes_of(c, b * BLOCK, BLOCK)
+            inside = lanes_of(c, (b + 1) * BLOCK, BLOCK)
+            outer = [
+                rim[core, mirrored(at, 3), :, outside].astype(f32) * outer_weight
+                for at in range(4)
+            ]
+            middle = [own[mirrored(at, 2), :, inside].astype(f32) for at in range(PLANES)]
+            inner = [rim[1 - core, mirrored(at, 3), :, outside].astype(f32) for at in range(4)]
+            stack = outer + middle + inner[:3] + [inner[3] * inner_weight]
+            for q in range(PLANES):
+                p = mirrored(q, 2)
+                across = stack[q + 5] + stack[q + 3]
+                for offset in range(2, 5):
+                    across = across + scaled_coeffs[offset] * (
+                        stack[q + 4 + offset] + stack[q + 4 - offset]
+                    )
+                at = 16 * (q * PER_CHUNK + b)
+                across = gain * (across + flat[slot, at : at + 16])
+                for half in range(2):
+                    lanes = lanes_of(c, half * FOLD + b * BLOCK, BLOCK)
+                    centre = source[p, :, lanes]
+                    factor = pot_ref[pl.ds(p, 1), lanes] * (1.0 / energy_scale) + level
+                    value = centre * factor - across[8 * half : 8 * half + 8]
+                    finish(p, b, half, lanes, centre, value)
+
+    def sweep(phase, use):
+        receive(phase, 0)
+
+        def step(c, carry):
+            @pl.when(c < CHUNKS)
+            def _():
+                receive(phase, c)
+
+            use(c - 1)
+            return carry
+
+        lax.fori_loop(1, CHUNKS + 1, step, 0)
+
+
+    def first_chunk(c):
         values = []
 
         def finish(p, b, half, lanes, centre, value):
@@ -324,9 +332,8 @@
         stencil(0, field, c, finish)
         for kind in range(3):
             halo(1, kind, c).start()
-        return carry
-
-    lax.fori_loop(0, CHUNKS, first_chunk, 0)
+
+    sweep(0, first_chunk)
     pl.semaphore_wait(hand.at[0], 2)
     greet(hand.at[2], "band", z, BAND, 4)
     pl.semaphore_wait(hand.at[1], 2)
@@ -347,7 +354,7 @@
             store_sem.at[c, half, part],
         )
 
-    def second_chunk(c, carry):
+    def second_chunk(c):
         def finish(p, b, half, lanes, centre, value):
             swapped = jnp.concatenate([centre[4:8], centre[0:4]], axis=0)
             result = (
@@ -363,16 +370,15 @@
         for half in range(2):
             for part in range(2):
                 stores(c, half, part).start()
-        return carry
-
-    lax.fori_loop(0, CHUNKS, second_chunk, 0)
+
+    sweep(1, second_chunk)
     pl.semaphore_wait(hand.at[2], 2)
     pl.semaphore_wait(hand.at[3], 2)
     greet(hand.at[4], "space", s, SPACE, 8)
 
     for copy in tables[1:]:
         copy.wait()
-    turned = exact_dot(lines[...], fz_ref[...])
+    turned = exact_dot(lines[...], forward_ref[0:BLOCK, :])
     stacked = jnp.concatenate(
         [
             jnp.concatenate(
@@ -386,7 +392,7 @@
         ],
         axis=1,
     )
-    spectral = exact_dot(fy_ref[...], stacked)
+    spectral = exact_dot(forward_ref[BLOCK : BLOCK + NY, 0:NY], stacked)
     lane = lax.broadcasted_iota(jnp.int32, (1, 128), 1)
     for p in range(PLANES):
         wide = spectral[:, p * 256 : p * 256 + 128]
@@ -528,9 +534,11 @@
             pieces += [jnp.concatenate(upper, axis=0), jnp.concatenate(lower, axis=0)]
         spread = jnp.concatenate(pieces, axis=1).astype(bf16)
         rows_y = jnp.dot(
-            iy_ref[...], jnp.concatenate([spread, spread], axis=0), preferred_element_type=f32
-        )
-        flat = jnp.concatenate(
+            inverse_ref[2048 : 2048 + NY, 0 : 2 * NY],
+            jnp.concatenate([spread, spread], axis=0),
+            preferred_element_type=f32,
+        )
+        wide = jnp.concatenate(
             [
                 jnp.concatenate(
                     [
@@ -543,13 +551,13 @@
             ],
             axis=0,
         )
-        high = flat.astype(bf16)
-        low = (flat - high.astype(f32)).astype(bf16)
-        z_high = iz_ref[0:1024]
+        high = wide.astype(bf16)
+        low = (wide - high.astype(f32)).astype(bf16)
+        z_high = inverse_ref[0:1024]
         return (
             jnp.dot(high, z_high, preferred_element_type=f32)
             + jnp.dot(low, z_high, preferred_element_type=f32)
-            + jnp.dot(high, iz_ref[1024:2048], preferred_element_type=f32)
+            + jnp.dot(high, inverse_ref[1024:2048], preferred_element_type=f32)
         )
 
     def put(out_ref, values):
@@ -564,8 +572,8 @@
             def _():
                 pltpu.make_async_copy(dens_own, dst.at[o], recv.at[o]).wait()
 
-    dens_copy = pltpu.make_async_copy(dens_ref, dens_hbm, table_sem.at[8])
-    hart_copy = pltpu.make_async_copy(hart_ref, hart_hbm, table_sem.at[9])
+    dens_copy = pltpu.make_async_copy(dens_ref, dens_hbm, table_sem.at[6])
+    hart_copy = pltpu.make_async_copy(hart_ref, hart_hbm, table_sem.at[7])
     gathered(dens_modes, dens_recv)
     put(dens_ref, back(dens_modes))
     dens_copy.start()
@@ -626,7 +634,7 @@
 def per_device(orbitals, potential, occupations):
     f32 = jnp.float32
     bf16 = jnp.bfloat16
-    forward_z, forward_y, inverse_y, inverse_z, green = transform_tables()
+    forward, inverse, green = transform_tables()
     vmem = pltpu.VMEM
     dma = pltpu.SemaphoreType.DMA
     anywhere = pl.BlockSpec(memory_space=pl.ANY)
@@ -637,13 +645,14 @@
             jax.ShapeDtypeStruct((PLANES, CELLS), f32),
             jax.ShapeDtypeStruct((PLANES, CELLS), f32),
         ),
-        in_specs=[anywhere] * 9,
+        in_specs=[anywhere] * 7,
         out_specs=(anywhere, anywhere, anywhere),
         scratch_shapes=[
             vmem((PLANES, CELLS), f32),
             pltpu.SMEM((4,), f32),
             vmem((PLANES, CELLS), f32),
             vmem((PLANES, CELLS), f32),
+            vmem((2, 16 * PLANES * PER_CHUNK, BLOCK), f32),
             vmem((PLANES, FIELDS, CELLS), f32),
             vmem((PLANES, FIELDS, CELLS), f32),
             vmem((PLANES, FIELDS, CELLS), f32),
@@ -653,10 +662,8 @@
             vmem((2, 4, 16, FOLD), bf16),
             vmem((PLANES * BLOCKS, BLOCK), f32),
             vmem((WINDOW, BLOCK), bf16),
-            vmem((BLOCK, 1024), f32),
-            vmem((NY, NY), f32),
-            vmem((NY, 2 * NY), bf16),
-            vmem((2048, BLOCK), bf16),
+            vmem((BLOCK + NY, 1024), f32),
+            vmem((2048 + NY, BLOCK), bf16),
             vmem((NX + 5, 8, 128), f32),
             vmem((OWNERS, PLANES, 8, 128), f32),
             vmem((BAND, PLANES, 8, 128), f32),
@@ -669,7 +676,7 @@
             vmem((OWNERS, 2, 16, 128), bf16),
             vmem((OWNERS, 2, 16, 128), bf16),
             dma((CHUNKS, 2, 2)),
-            dma((10,)),
+            dma((8,)),
             dma((CHUNKS, 2, 2)),
             dma((2, 4, CHUNKS)),
             dma((2, 4, CHUNKS)),
@@ -692,10 +699,8 @@
         potential,
         occupations,
         jnp.asarray(band_matrix()),
-        jnp.asarray(forward_z),
-        jnp.asarray(forward_y),
-        jnp.asarray(inverse_y),
-        jnp.asarray(inverse_z),
+        jnp.asarray(forward),
+        jnp.asarray(inverse),
         jnp.asarray(green),
     )
     prop, dens, hart = pl.pallas_call(

time: 61.8 us -> 61.5 us (level)
  no operation moved by 1% of the time
where the time goes in v4:
time: 61.5 us; the launch traced here: 61.3 us
  Pallas kernels  60.7 us (99%)
  between operations  0.64 us (1%)
    pallas_call x1, Pallas kernels, per_device(): pl.pallas_call(body, out_shape=(jax.ShapeDtypeStruct((2, PLANES, 4, CELLS...  58.5 us
    pallas_call x1, Pallas kernels, per_device(): pl.pallas_call(settle, out_shape=[jax.ShapeDtypeStruct(r.shape, r.dtype)...  2.15 us

profile of v4, /device:TPU:1, one launch (start us, length us, event | category | flops | bytes accessed | tf_op | source)
XLA Modules:
  0.0 61.3 jit_solution(16271057135215180820)
XLA Ops:
  0.6 58.5 %shard_map.94 = (f32[2,3,4,9216]{3,2,1,0:T(4,128)}, f32[3,9216]{1,0:T(4,128)}, f32[3,9216]{1,0:T(4,128)}) custom-call(f32[2,3,4,9216]{3,2,1,0:T(4,128)} %bitcast.2, f32[3,9216]{1,0:T(4,128)} %pot_hbm.1, f32[4]{0:T(128)} %occ_hbm.1, bf16[1152,384]{1,0:T(8,128)(2,1)} %constant.8.clone.band_hbm, f32[480,1024]{1,0:T(8,128)} %constant.9.clone.forward_hbm, ...), custom_call_target="tpu_custom_call" | custom-call | tf_op jit(solution)/shard_map/pallas_call | solution.py:641
  59.2 2.1 %shard_map.95 = (f32[2,3,4,9216]{3,2,1,0:T(4,128)}, f32[3,9216]{1,0:T(4,128)}, f32[3,9216]{1,0:T(4,128)}) custom-call(f32[2,3,4,9216]{3,2,1,0:T(4,128)} %get-tuple-element.9.prop_in, f32[3,9216]{1,0:T(4,128)} %get-tuple-element.10.dens_in, f32[3,9216]{1,0:T(4,128)} %get-tuple-element.11.hart_in), custom_call_target="tpu_custom_call" | custom-call | tf_op jit(solution)/shard_map/pallas_call | solution.py:706

commit v5 on v4

--- a/solution.py
+++ b/solution.py
@@ -78,11 +78,10 @@
     order = np.array([4 * block + r for r in range(4) for block in range(BLOCKS)])
     forward_y = basis[:, order]
     lanes = np.arange(128)
-    spread = np.stack([basis[lanes % 64], basis[64 + lanes % 32]])
-    forward_z = np.zeros((4, NZ, 4, 2, 128))
+    forward_z = np.zeros((4, NZ, 4, 128))
     for r in range(4):
-        forward_z[r, :, r] = np.transpose(spread, (2, 0, 1))
-    forward_z = forward_z.reshape(BLOCK, 1024)
+        forward_z[r, :, r, :NZ] = basis.T
+    forward_z = forward_z.reshape(BLOCK, 512)
     row = np.arange(72)[:, None]
     mode_y = np.where(row < 48, row + 48 * (lanes >= 64), row - 48 + 24 * (lanes // 32))
     mode_z = np.where(row < 48, lanes % 64, 64 + lanes % 32)
@@ -99,7 +98,7 @@
     y_high, y_low = split(forward_y.T)
     z_high, z_low = split(forward_z.T)
     return (
-        np.concatenate([forward_z, np.pad(forward_y, ((0, 0), (0, 1024 - NY)))]).astype(f32),
+        np.concatenate([forward_z, np.pad(forward_y, ((0, 0), (0, 512 - NY)))]).astype(f32),
         np.concatenate([z_high, z_low, np.pad(np.concatenate([y_high, y_low], axis=1), ((0, 0), (0, BLOCK - 2 * NY)))]),
         green.astype(f32),
     )
@@ -383,7 +382,7 @@
         [
             jnp.concatenate(
                 [
-                    turned[p * BLOCKS : (p + 1) * BLOCKS, r * 256 : (r + 1) * 256]
+                    turned[p * BLOCKS : (p + 1) * BLOCKS, r * 128 : (r + 1) * 128]
                     for r in range(4)
                 ],
                 axis=0,
@@ -395,12 +394,14 @@
     spectral = exact_dot(forward_ref[BLOCK : BLOCK + NY, 0:NY], stacked)
     lane = lax.broadcasted_iota(jnp.int32, (1, 128), 1)
     for p in range(PLANES):
-        wide = spectral[:, p * 256 : p * 256 + 128]
-        tail = spectral[:, p * 256 + 128 : (p + 1) * 256]
-        head = jnp.where(lane < 64, wide[0:48], wide[48:96])
-        rest = tail[0:24]
+        full = spectral[:, p * 128 : (p + 1) * 128]
+        head = jnp.where(lane < 64, full[0:48], pltpu.roll(full[48:96], 64, 1))
+        rest = pltpu.roll(full[0:24], 64, 1)
         for quarter in range(1, 4):
-            rest = jnp.where(lane >= 32 * quarter, tail[24 * quarter : 24 * quarter + 24], rest)
+            piece = full[24 * quarter : 24 * quarter + 24]
+            turn = (32 * quarter + 64) % 128
+            piece = pltpu.roll(piece, turn, 1) if turn else piece
+            rest = jnp.where(lane >= 32 * quarter, piece, rest)
         for o in range(6):
             modes[o, p] = head[8 * o : 8 * o + 8]
         for o in range(3):
@@ -529,12 +530,15 @@
             blocks = [halves[o][p // 2][at : at + 8] for o in range(OWNERS)]
             head = jnp.concatenate(blocks[:6], axis=0)
             rest = jnp.concatenate(blocks[6:], axis=0)
-            upper = [jnp.where(lane < 64, head, 0.0), jnp.where(lane >= 64, head, 0.0)]
-            lower = [jnp.where(lane // 32 == quarter, rest, 0.0) for quarter in range(4)]
-            pieces += [jnp.concatenate(upper, axis=0), jnp.concatenate(lower, axis=0)]
+            upper = jnp.concatenate([head, pltpu.roll(head, 64, 1)], axis=0)
+            lower = jnp.concatenate(
+                [pltpu.roll(rest, 64, 1), pltpu.roll(rest, 32, 1), rest, pltpu.roll(rest, 96, 1)],
+                axis=0,
+            )
+            pieces.append(jnp.where(lane < 64, upper, jnp.where(lane < NZ, lower, 0.0)))
         spread = jnp.concatenate(pieces, axis=1).astype(bf16)
         rows_y = jnp.dot(
-            inverse_ref[2048 : 2048 + NY, 0 : 2 * NY],
+            inverse_ref[1024 : 1024 + NY, 0 : 2 * NY],
             jnp.concatenate([spread, spread], axis=0),
             preferred_element_type=f32,
         )
@@ -542,7 +546,7 @@
             [
                 jnp.concatenate(
                     [
-                        rows_y[r * BLOCKS : (r + 1) * BLOCKS, p * 256 : (p + 1) * 256]
+                        rows_y[r * BLOCKS : (r + 1) * BLOCKS, p * 128 : (p + 1) * 128]
                         for r in range(4)
                     ],
                     axis=1,
@@ -553,11 +557,11 @@
         )
         high = wide.astype(bf16)
         low = (wide - high.astype(f32)).astype(bf16)
-        z_high = inverse_ref[0:1024]
+        z_high = inverse_ref[0:512]
         return (
             jnp.dot(high, z_high, preferred_element_type=f32)
             + jnp.dot(low, z_high, preferred_element_type=f32)
-            + jnp.dot(high, inverse_ref[1024:2048], preferred_element_type=f32)
+            + jnp.dot(high, inverse_ref[512:1024], preferred_element_type=f32)
         )
 
     def put(out_ref, values):
@@ -577,9 +581,6 @@
     gathered(dens_modes, dens_recv)
     put(dens_ref, back(dens_modes))
     dens_copy.start()
-    gathered(hart_modes, hart_recv)
-    put(hart_ref, back(hart_modes))
-    hart_copy.start()
 
     @pl.when(is_owner)
     def _():
@@ -589,12 +590,11 @@
 
         lax.fori_loop(1, SPACE // 2, drain_layer, 0)
 
-        def drain_band(k, carry):
+        def drain_dens(k, carry):
             band_copy(dens_own, dens_modes, dens_send, dens_recv, k).wait_send()
-            band_copy(hart_own, hart_modes, hart_send, hart_recv, k).wait_send()
             return carry
 
-        lax.fori_loop(1, BAND, drain_band, 0)
+        lax.fori_loop(1, BAND, drain_dens, 0)
 
     for o in range(OWNERS):
         @pl.when((BAND * o) // OWNERS != z)
@@ -612,6 +612,18 @@
 
     lax.fori_loop(0, CHUNKS, drain, 0)
     dens_copy.wait()
+    gathered(hart_modes, hart_recv)
+    put(hart_ref, back(hart_modes))
+    hart_copy.start()
+
+    @pl.when(is_owner)
+    def _():
+        def drain_hart(k, carry):
+            band_copy(hart_own, hart_modes, hart_send, hart_recv, k).wait_send()
+            return carry
+
+        lax.fori_loop(1, BAND, drain_hart, 0)
+
     hart_copy.wait()
 
 
@@ -662,8 +674,8 @@
             vmem((2, 4, 16, FOLD), bf16),
             vmem((PLANES * BLOCKS, BLOCK), f32),
             vmem((WINDOW, BLOCK), bf16),
-            vmem((BLOCK + NY, 1024), f32),
-            vmem((2048 + NY, BLOCK), bf16),
+            vmem((BLOCK + NY, 512), f32),
+            vmem((1024 + NY, BLOCK), bf16),
             vmem((NX + 5, 8, 128), f32),
             vmem((OWNERS, PLANES, 8, 128), f32),
             vmem((BAND, PLANES, 8, 128), f32),

time: 61.5 us -> 60.9 us (level)
  no operation moved by 1% of the time
where the time goes in v5:
time: 60.9 us; the launch traced here: 60.7 us
  Pallas kernels  60.1 us (99%)
  between operations  0.64 us (1%)
    pallas_call x1, Pallas kernels, per_device(): pl.pallas_call(body, out_shape=(jax.ShapeDtypeStruct((2, PLANES, 4, CELLS...  57.9 us
    pallas_call x1, Pallas kernels, per_device(): pl.pallas_call(settle, out_shape=[jax.ShapeDtypeStruct(r.shape, r.dtype)...  2.15 us

profile of v5, /device:TPU:1, one launch (start us, length us, event | category | flops | bytes accessed | tf_op | source)
XLA Modules:
  0.0 60.7 jit_solution(6484343325384063392)
XLA Ops:
  0.6 57.9 %shard_map.94 = (f32[2,3,4,9216]{3,2,1,0:T(4,128)}, f32[3,9216]{1,0:T(4,128)}, f32[3,9216]{1,0:T(4,128)}) custom-call(f32[2,3,4,9216]{3,2,1,0:T(4,128)} %bitcast.2, f32[3,9216]{1,0:T(4,128)} %pot_hbm.1, f32[4]{0:T(128)} %occ_hbm.1, bf16[1152,384]{1,0:T(8,128)(2,1)} %constant.8.clone.band_hbm, f32[480,512]{1,0:T(8,128)} %constant.9.clone.forward_hbm, ...), custom_call_target="tpu_custom_call" | custom-call | tf_op jit(solution)/shard_map/pallas_call | solution.py:653
  58.6 2.1 %shard_map.95 = (f32[2,3,4,9216]{3,2,1,0:T(4,128)}, f32[3,9216]{1,0:T(4,128)}, f32[3,9216]{1,0:T(4,128)}) custom-call(f32[2,3,4,9216]{3,2,1,0:T(4,128)} %get-tuple-element.9.prop_in, f32[3,9216]{1,0:T(4,128)} %get-tuple-element.10.dens_in, f32[3,9216]{1,0:T(4,128)} %get-tuple-element.11.hart_in), custom_call_target="tpu_custom_call" | custom-call | tf_op jit(solution)/shard_map/pallas_call | solution.py:718

commit v6 on v5

--- a/solution.py
+++ b/solution.py
@@ -27,7 +27,7 @@
 FOLD = CELLS // 2
 BLOCK = 4 * NZ
 BLOCKS = CELLS // BLOCK
-CHUNKS = 4
+CHUNKS = 6
 CHUNK = FOLD // CHUNKS
 PER_CHUNK = CHUNK // BLOCK
 WINDOW = 3 * BLOCK

time: 60.9 us -> 61.7 us (1.013)
  Pallas kernels: 60.1 us -> 60.9 us
    pallas_call x1, Pallas kernels: 57.9 us -> 58.7 us  [per_device(): pl.pallas_call(body, out_shape=(jax.ShapeDtypeStruct((2, PLANES, 4, CELLS...]
where the time goes in v6:
time: 61.7 us; the launch traced here: 61.5 us
  Pallas kernels  60.9 us (99%)
  between operations  0.64 us (1%)
    pallas_call x1, Pallas kernels, per_device(): pl.pallas_call(body, out_shape=(jax.ShapeDtypeStruct((2, PLANES, 4, CELLS...  58.7 us
    pallas_call x1, Pallas kernels, per_device(): pl.pallas_call(settle, out_shape=[jax.ShapeDtypeStruct(r.shape, r.dtype)...  2.15 us

profile of v6, /device:TPU:1, one launch (start us, length us, event | category | flops | bytes accessed | tf_op | source)
XLA Modules:
  0.0 61.5 jit_solution(3842163661499229264)
XLA Ops:
  0.6 58.7 %shard_map.94 = (f32[2,3,4,9216]{3,2,1,0:T(4,128)}, f32[3,9216]{1,0:T(4,128)}, f32[3,9216]{1,0:T(4,128)}) custom-call(f32[2,3,4,9216]{3,2,1,0:T(4,128)} %bitcast.2, f32[3,9216]{1,0:T(4,128)} %pot_hbm.1, f32[4]{0:T(128)} %occ_hbm.1, bf16[1152,384]{1,0:T(8,128)(2,1)} %constant.8.clone.band_hbm, f32[480,512]{1,0:T(8,128)} %constant.9.clone.forward_hbm, ...), custom_call_target="tpu_custom_call" | custom-call | tf_op jit(solution)/shard_map/pallas_call | solution.py:653
  59.4 2.1 %shard_map.95 = (f32[2,3,4,9216]{3,2,1,0:T(4,128)}, f32[3,9216]{1,0:T(4,128)}, f32[3,9216]{1,0:T(4,128)}) custom-call(f32[2,3,4,9216]{3,2,1,0:T(4,128)} %get-tuple-element.9.prop_in, f32[3,9216]{1,0:T(4,128)} %get-tuple-element.10.dens_in, f32[3,9216]{1,0:T(4,128)} %get-tuple-element.11.hart_in), custom_call_target="tpu_custom_call" | custom-call | tf_op jit(solution)/shard_map/pallas_call | solution.py:718

commit v7 on v5

--- a/solution.py
+++ b/solution.py
@@ -95,23 +95,32 @@
     green = green[(np.arange(NX + 5) - 5) % NX]
     green = green.reshape(NX + 5, OWNERS, 8, 128).transpose(1, 0, 2, 3)
     f32 = np.float32
+    forward = np.concatenate([forward_z, np.pad(forward_y, ((0, 0), (0, 512 - NY)))])
+    f_high, f_middle = split(forward)
+    f_low = split(forward - f_high.astype(np.float64))[1]
     y_high, y_low = split(forward_y.T)
     z_high, z_low = split(forward_z.T)
     return (
-        np.concatenate([forward_z, np.pad(forward_y, ((0, 0), (0, 512 - NY)))]).astype(f32),
+        np.stack([f_high, f_middle, f_low]),
         np.concatenate([z_high, z_low, np.pad(np.concatenate([y_high, y_low], axis=1), ((0, 0), (0, BLOCK - 2 * NY)))]),
         green.astype(f32),
     )
 
 
+def thirds(values):
+    f32, bf16 = jnp.float32, jnp.bfloat16
+    high = values.astype(bf16)
+    rest = values - high.astype(f32)
+    middle = rest.astype(bf16)
+    return high, middle, (rest - middle.astype(f32)).astype(bf16)
+
+
 def exact_dot(a, b):
-    return lax.dot_general(
-        a,
-        b,
-        (((1,), (0,)), ((), ())),
-        precision=lax.Precision.HIGHEST,
-        preferred_element_type=jnp.float32,
-    )
+    def one(i, j):
+        return jnp.dot(a[i], b[j], preferred_element_type=jnp.float32)
+
+    small = (one(0, 2) + one(2, 0)) + one(1, 1)
+    return (small + (one(0, 1) + one(1, 0))) + one(0, 0)
 
 
 def body(
@@ -377,7 +386,7 @@
 
     for copy in tables[1:]:
         copy.wait()
-    turned = exact_dot(lines[...], forward_ref[0:BLOCK, :])
+    turned = exact_dot(thirds(lines[...]), [forward_ref[i, 0:BLOCK, :] for i in range(3)])
     stacked = jnp.concatenate(
         [
             jnp.concatenate(
@@ -391,7 +400,9 @@
         ],
         axis=1,
     )
-    spectral = exact_dot(forward_ref[BLOCK : BLOCK + NY, 0:NY], stacked)
+    spectral = exact_dot(
+        [forward_ref[i, BLOCK : BLOCK + NY, 0:NY] for i in range(3)], thirds(stacked)
+    )
     lane = lax.broadcasted_iota(jnp.int32, (1, 128), 1)
     for p in range(PLANES):
         full = spectral[:, p * 128 : (p + 1) * 128]
@@ -674,7 +685,7 @@
             vmem((2, 4, 16, FOLD), bf16),
             vmem((PLANES * BLOCKS, BLOCK), f32),
             vmem((WINDOW, BLOCK), bf16),
-            vmem((BLOCK + NY, 512), f32),
+            vmem((3, BLOCK + NY, 512), bf16),
             vmem((1024 + NY, BLOCK), bf16),
             vmem((NX + 5, 8, 128), f32),
             vmem((OWNERS, PLANES, 8, 128), f32),

time: 60.9 us -> 60.8 us (level)
  no operation moved by 1% of the time
where the time goes in v7:
time: 60.8 us; the launch traced here: 60.7 us
  Pallas kernels  60 us (99%)
  between operations  0.64 us (1%)
    pallas_call x1, Pallas kernels, per_device(): pl.pallas_call(body, out_shape=(jax.ShapeDtypeStruct((2, PLANES, 4, CELLS...  57.9 us
    pallas_call x1, Pallas kernels, per_device(): pl.pallas_call(settle, out_shape=[jax.ShapeDtypeStruct(r.shape, r.dtype)...  2.15 us

profile of v7, /device:TPU:1, one launch (start us, length us, event | category | flops | bytes accessed | tf_op | source)
XLA Modules:
  0.0 60.7 jit_solution(5503371657703872272)
XLA Ops:
  0.6 57.9 %shard_map.94 = (f32[2,3,4,9216]{3,2,1,0:T(4,128)}, f32[3,9216]{1,0:T(4,128)}, f32[3,9216]{1,0:T(4,128)}) custom-call(f32[2,3,4,9216]{3,2,1,0:T(4,128)} %bitcast.2, f32[3,9216]{1,0:T(4,128)} %pot_hbm.1, f32[4]{0:T(128)} %occ_hbm.1, bf16[1152,384]{1,0:T(8,128)(2,1)} %constant.8.clone.band_hbm, bf16[3,480,512]{2,1,0:T(8,128)(2,1)} %constant.9.clone.forward_hbm, ...), custom_call_target="tpu_custom_call" | custom-call | tf_op jit(solution)/shard_map/pallas_call | solution.py:664
  58.5 2.1 %shard_map.95 = (f32[2,3,4,9216]{3,2,1,0:T(4,128)}, f32[3,9216]{1,0:T(4,128)}, f32[3,9216]{1,0:T(4,128)}) custom-call(f32[2,3,4,9216]{3,2,1,0:T(4,128)} %get-tuple-element.9.prop_in, f32[3,9216]{1,0:T(4,128)} %get-tuple-element.10.dens_in, f32[3,9216]{1,0:T(4,128)} %get-tuple-element.11.hart_in), custom_call_target="tpu_custom_call" | custom-call | tf_op jit(solution)/shard_map/pallas_call | solution.py:729

commit v8 on v5

--- a/solution.py
+++ b/solution.py
@@ -233,7 +233,7 @@
     pl.semaphore_wait(barrier, 8)
 
     def ship(c, carry):
-        for kind in range(3):
+        for kind in (0, 2, 1):
             halo(0, kind, c).start()
         return carry
 
@@ -329,7 +329,7 @@
                 ).astype(bf16)
 
         stencil(0, field, c, finish)
-        for kind in range(3):
+        for kind in (0, 2, 1):
             halo(1, kind, c).start()
 
     sweep(0, first_chunk)

time: 60.9 us -> 60.9 us (level)
  no operation moved by 1% of the time
where the time goes in v8:
time: 60.9 us; the launch traced here: 60.7 us
  Pallas kernels  60.1 us (99%)
  between operations  0.64 us (1%)
    pallas_call x1, Pallas kernels, per_device(): pl.pallas_call(body, out_shape=(jax.ShapeDtypeStruct((2, PLANES, 4, CELLS...  57.9 us
    pallas_call x1, Pallas kernels, per_device(): pl.pallas_call(settle, out_shape=[jax.ShapeDtypeStruct(r.shape, r.dtype)...  2.15 us

profile of v8, /device:TPU:1, one launch (start us, length us, event | category | flops | bytes accessed | tf_op | source)
XLA Modules:
  0.0 60.7 jit_solution(11192146941407236771)
XLA Ops:
  0.6 57.9 %shard_map.94 = (f32[2,3,4,9216]{3,2,1,0:T(4,128)}, f32[3,9216]{1,0:T(4,128)}, f32[3,9216]{1,0:T(4,128)}) custom-call(f32[2,3,4,9216]{3,2,1,0:T(4,128)} %bitcast.2, f32[3,9216]{1,0:T(4,128)} %pot_hbm.1, f32[4]{0:T(128)} %occ_hbm.1, bf16[1152,384]{1,0:T(8,128)(2,1)} %constant.8.clone.band_hbm, f32[480,512]{1,0:T(8,128)} %constant.9.clone.forward_hbm, ...), custom_call_target="tpu_custom_call" | custom-call | tf_op jit(solution)/shard_map/pallas_call | solution.py:653
  58.6 2.1 %shard_map.95 = (f32[2,3,4,9216]{3,2,1,0:T(4,128)}, f32[3,9216]{1,0:T(4,128)}, f32[3,9216]{1,0:T(4,128)}) custom-call(f32[2,3,4,9216]{3,2,1,0:T(4,128)} %get-tuple-element.9.prop_in, f32[3,9216]{1,0:T(4,128)} %get-tuple-element.10.dens_in, f32[3,9216]{1,0:T(4,128)} %get-tuple-element.11.hart_in), custom_call_target="tpu_custom_call" | custom-call | tf_op jit(solution)/shard_map/pallas_call | solution.py:718
